TPU v7x, 32 devices: a whole 2x2x4 slice. The times are simulated.
32 devices in a mesh: wide: 8 (over y, x, core), narrow: 4 (over z).
Axes of the slice: x: 2, y: 2, z: 4, core: 2. Of those that a mesh axis runs over, the one named last changes fastest.
Arguments:
- tokens: bfloat16 [8192, 1024], P('wide', 'narrow'), may hold values from -6 to 6
- segments: int32 [8192], P('wide'), may hold values from 0 to 15, as said below
- first_gain: bfloat16 [1024], P('narrow'), may hold values from 0.25 to 1.75
- first_shift: bfloat16 [1024], P('narrow'), may hold values from -1.75 to 1.75
- qkv_weight: bfloat16 [1024, 3072], P('wide', 'narrow'), may hold values from -0.1875 to 0.1875
- qv_bias: bfloat16 [2048], P('narrow'), may hold values from -1.75 to 1.75
- dense_weight: bfloat16 [1024, 1024], P('narrow', 'wide'), may hold values from -0.5 to 0.5
- dense_bias: bfloat16 [1024], P('narrow'), may hold values from -1.75 to 1.75
- second_gain: bfloat16 [1024], P('narrow'), may hold values from 0.25 to 1.75
- second_shift: bfloat16 [1024], P('narrow'), may hold values from -1.75 to 1.75
- up_weight: bfloat16 [1024, 4096], P('wide', 'narrow'), may hold values from -0.1875 to 0.1875
- up_bias: bfloat16 [4096], P('narrow'), may hold values from -1.75 to 1.75
- down_weight: bfloat16 [4096, 1024], P('narrow', 'wide'), may hold values from -0.09375 to 0.09375
- down_bias: bfloat16 [1024], P('narrow'), may hold values from -1.75 to 1.75
- cotangent: bfloat16 [8192, 1024], P('wide', 'narrow'), may hold values from -8 to 8
Outputs:
- output: bfloat16 [8192, 1024], P('wide', 'narrow')
- token_grad: bfloat16 [8192, 1024], P('wide', 'narrow')
- first_gain_grad: float32 [1024], P('narrow')
- first_shift_grad: float32 [1024], P('narrow')
- qkv_weight_grad: float32 [1024, 3072], P('wide', 'narrow')
- qv_bias_grad: float32 [2048], P('narrow')
- dense_weight_grad: float32 [1024, 1024], P('narrow', 'wide')
- dense_bias_grad: float32 [1024], P('narrow')
- second_gain_grad: float32 [1024], P('narrow')
- second_shift_grad: float32 [1024], P('narrow')
- up_weight_grad: float32 [1024, 4096], P('wide', 'narrow')
- up_bias_grad: float32 [4096], P('narrow')
- down_weight_grad: float32 [4096, 1024], P('narrow', 'wide')
- down_bias_grad: float32 [1024], P('narrow')
Inputs may be any that keep to these rules, and one draw needn't show every extreme that they name: `segments`: every aligned block b of 1024 positions holds either one whole sequence numbered 2 b, or two sequences of 512 positions numbered 2 b and 2 b + 1; the last block always holds two.
All inputs are finite; a program needn't handle non-finite values.
Results may differ from a plain program's by a relative error of at most 0.018.
Values may be sent and summed in bfloat16 or wider, within the bound.
A program may use at most 128 MiB of HBM per device.

v0:
```python
from functools import partial

import jax
import jax.numpy as jnp
from jax import lax
from jax.sharding import PartitionSpec as P

H = 16
HD = 64


eps = 1e-05
negative = -1e30
block_rows = 512


def normalize(values, gain, shift):
    mean_value = jnp.mean(values, axis=-1, keepdims=True)
    centered = values - mean_value
    inv_std = lax.rsqrt(jnp.mean(centered * centered, axis=-1, keepdims=True) + eps)
    normed = centered * inv_std
    return (normed * gain + shift, normed, inv_std)


def norm_backward(grad_norm, gain, normed, inv_std):
    scaled = grad_norm * gain
    mean_one = jnp.mean(scaled, axis=-1, keepdims=True)
    mean_two = jnp.mean(scaled * normed, axis=-1, keepdims=True)
    return inv_std * (scaled - mean_one - normed * mean_two)


def own_columns(values, col_start, local_width):
    return lax.dynamic_slice_in_dim(values, col_start, local_width, values.ndim - 1)


def masked_scores(query_block, key_block, slope, query_pos, key_pos, query_seg, key_seg):
    logits = jnp.einsum(
        "qd,kd->qk", query_block, key_block, preferred_element_type=jnp.float32
    ) * HD ** (-0.5)
    logits = logits - slope * (query_pos[:, None] - key_pos[None, :]).astype(jnp.float32)
    allowed = (key_pos[None, :] <= query_pos[:, None]) & (query_seg[:, None] == key_seg[None, :])
    return jnp.where(allowed, logits, negative)


def attend_forward(query, keys, values, slopes, positions, segments):
    tok_rows = query.shape[1]
    step_rows = min(block_rows, tok_rows)
    outputs = []
    totals = []
    for row_start in range(0, tok_rows, step_rows):
        row_end = row_start + step_rows

        def one_head(operands):
            query_head, key_head, value_head, slope = operands
            logits = masked_scores(
                query_head[row_start:row_end],
                key_head[:row_end],
                slope,
                positions[row_start:row_end],
                positions[:row_end],
                segments[row_start:row_end],
                segments[:row_end],
            )
            top_score = jnp.max(logits, axis=-1, keepdims=True)
            log_total = top_score + jnp.log(
                jnp.sum(jnp.exp(logits - top_score), axis=-1, keepdims=True)
            )
            probs = jnp.exp(logits - log_total).astype(jnp.bfloat16)
            return (
                jnp.dot(probs, value_head[:row_end], preferred_element_type=jnp.float32),
                log_total[:, 0],
            )

        head_out, head_total = lax.map(one_head, (query, keys, values, slopes))
        outputs.append(head_out)
        totals.append(head_total)
    return (jnp.concatenate(outputs, axis=1), jnp.concatenate(totals, axis=1))


def attend_backward(query, keys, values, slopes, positions, segments, log_totals, grad_heads):
    tok_rows = query.shape[1]
    step_rows = min(block_rows, tok_rows)
    grad_queries = []
    grad_keys = jnp.zeros(query.shape, jnp.float32)
    grad_values = jnp.zeros(query.shape, jnp.float32)
    for row_start in range(0, tok_rows, step_rows):
        row_end = row_start + step_rows

        def one_head(operands):
            query_head, key_head, value_head, slope, log_head, grad_head = operands
            logits = masked_scores(
                query_head[row_start:row_end],
                key_head[:row_end],
                slope,
                positions[row_start:row_end],
                positions[:row_end],
                segments[row_start:row_end],
                segments[:row_end],
            )
            probs = jnp.exp(logits - log_head[row_start:row_end, None])
            grad_block = grad_head[row_start:row_end]
            grad_probs = jnp.einsum(
                "qd,kd->qk", grad_block, value_head[:row_end], preferred_element_type=jnp.float32
            )
            weighted = jnp.sum(probs * grad_probs, axis=-1, keepdims=True)
            grad_logits = (probs * (grad_probs - weighted)).astype(jnp.bfloat16)
            grad_query = HD ** (-0.5) * jnp.dot(
                grad_logits, key_head[:row_end], preferred_element_type=jnp.float32
            )
            grad_key = HD ** (-0.5) * jnp.einsum(
                "qk,qd->kd",
                grad_logits,
                query_head[row_start:row_end],
                preferred_element_type=jnp.float32,
            )
            grad_value = jnp.einsum(
                "qk,qd->kd",
                probs.astype(jnp.bfloat16),
                grad_block,
                preferred_element_type=jnp.float32,
            )
            return (grad_query, grad_key, grad_value)

        head_query, head_key, head_value = lax.map(
            one_head, (query, keys, values, slopes, log_totals, grad_heads)
        )
        padding = ((0, 0), (0, tok_rows - row_end), (0, 0))
        grad_queries.append(head_query)
        grad_keys = grad_keys + jnp.pad(head_key, padding)
        grad_values = grad_values + jnp.pad(head_value, padding)
    return (jnp.concatenate(grad_queries, axis=1), grad_keys, grad_values)


def local(
    tokens,
    segments,
    first_gain,
    first_shift,
    qkv_weight,
    qv_bias,
    dense_weight,
    dense_bias,
    second_gain,
    second_shift,
    up_weight,
    up_bias,
    down_weight,
    down_bias,
    cotangent,
):
    tok_rows, local_width = tokens.shape
    col_start = lax.axis_index("narrow") * local_width
    heads_here = qv_bias.shape[0] // (2 * HD)
    head_first = lax.axis_index("narrow") * heads_here
    slopes = 2.0 ** (-8.0 * (head_first + jnp.arange(heads_here) + 1).astype(jnp.float32) / H)
    positions = jnp.arange(tok_rows)
    full_tokens, gain_one, shift_one, bias_dense, gain_two, shift_two = (
        lax.all_gather(tokens, "narrow", axis=1, tiled=True),
        lax.all_gather(first_gain, "narrow", axis=0, tiled=True),
        lax.all_gather(first_shift, "narrow", axis=0, tiled=True),
        lax.all_gather(dense_bias, "narrow", axis=0, tiled=True),
        lax.all_gather(second_gain, "narrow", axis=0, tiled=True),
        lax.all_gather(second_shift, "narrow", axis=0, tiled=True),
    )
    qkv_full, dense_full = (
        lax.all_gather(qkv_weight, "wide", axis=0, tiled=True),
        lax.all_gather(dense_weight, "wide", axis=1, tiled=True),
    )
    up_full, down_full = (
        lax.all_gather(up_weight, "wide", axis=0, tiled=True),
        lax.all_gather(down_weight, "wide", axis=1, tiled=True),
    )
    inputs = full_tokens.astype(jnp.float32)
    normed_one, hat_one, inv_one = normalize(
        inputs, gain_one.astype(jnp.float32), shift_one.astype(jnp.float32)
    )
    act_one = normed_one.astype(jnp.bfloat16)
    projected = jnp.dot(act_one, qkv_full, preferred_element_type=jnp.float32).reshape(
        tok_rows, heads_here, 3, HD
    )
    bias_pair = qv_bias.astype(jnp.float32).reshape(heads_here, 2, HD)
    full_bias = jnp.stack(
        [bias_pair[:, 0], jnp.zeros_like(bias_pair[:, 0]), bias_pair[:, 1]], axis=1
    )
    packed = (projected + full_bias[None]).astype(jnp.bfloat16)
    head_major = jnp.transpose(packed, (2, 1, 0, 3))
    query, keys, values = (head_major[0], head_major[1], head_major[2])
    attended_heads, log_totals = attend_forward(query, keys, values, slopes, positions, segments)
    attended = (
        jnp.transpose(attended_heads, (1, 0, 2))
        .reshape(tok_rows, heads_here * HD)
        .astype(jnp.bfloat16)
    )
    mixed = lax.psum(
        jnp.dot(attended, dense_full, preferred_element_type=jnp.float32).astype(jnp.bfloat16),
        "narrow",
    ).astype(jnp.float32)
    residual = inputs + (mixed + bias_dense.astype(jnp.float32))
    normed_two, hat_two, inv_two = normalize(
        residual, gain_two.astype(jnp.float32), shift_two.astype(jnp.float32)
    )
    act_two = normed_two.astype(jnp.bfloat16)
    pre_act = jnp.dot(act_two, up_full, preferred_element_type=jnp.float32) + up_bias.astype(
        jnp.float32
    )
    hidden = jax.nn.gelu(pre_act, approximate=True).astype(jnp.bfloat16)
    mlp_out = lax.psum_scatter(
        jnp.dot(hidden, down_full, preferred_element_type=jnp.float32).astype(jnp.bfloat16),
        "narrow",
        scatter_dimension=1,
        tiled=True,
    ).astype(jnp.float32)
    output = (
        own_columns(residual, col_start, local_width) + (mlp_out + down_bias.astype(jnp.float32))
    ).astype(jnp.bfloat16)
    grad_out = lax.all_gather(cotangent, "narrow", axis=1, tiled=True)
    grad_down = jnp.einsum("rf,rd->fd", hidden, grad_out, preferred_element_type=jnp.float32)
    down_bias_grad = jnp.sum(cotangent.astype(jnp.float32), axis=0)
    grad_hidden = jnp.einsum("rd,fd->rf", grad_out, down_full, preferred_element_type=jnp.float32)
    _, gelu_back = jax.vjp(partial(jax.nn.gelu, approximate=True), pre_act)
    grad_pre = gelu_back(grad_hidden)[0].astype(jnp.bfloat16)
    up_bias_grad = jnp.sum(grad_pre.astype(jnp.float32), axis=0)
    grad_up = jnp.einsum("rd,rf->df", act_two, grad_pre, preferred_element_type=jnp.float32)
    grad_act_two = lax.psum(
        jnp.einsum("rf,df->rd", grad_pre, up_full, preferred_element_type=jnp.float32).astype(
            jnp.bfloat16
        ),
        "narrow",
    ).astype(jnp.float32)
    gain_two_full = gain_two.astype(jnp.float32)
    second_gain_grad = own_columns(jnp.sum(grad_act_two * hat_two, axis=0), col_start, local_width)
    second_shift_grad = own_columns(jnp.sum(grad_act_two, axis=0), col_start, local_width)
    grad_residual = grad_out.astype(jnp.float32) + norm_backward(
        grad_act_two, gain_two_full, hat_two, inv_two
    )
    grad_branch = grad_residual.astype(jnp.bfloat16)
    dense_bias_grad = own_columns(
        jnp.sum(grad_branch.astype(jnp.float32), axis=0), col_start, local_width
    )
    grad_dense = jnp.einsum("rh,rd->hd", attended, grad_branch, preferred_element_type=jnp.float32)
    grad_attended = jnp.einsum(
        "rd,hd->rh", grad_branch, dense_full, preferred_element_type=jnp.float32
    ).astype(jnp.bfloat16)
    grad_heads = jnp.transpose(grad_attended.reshape(tok_rows, heads_here, HD), (1, 0, 2))
    grad_query, grad_key, grad_value = attend_backward(
        query, keys, values, slopes, positions, segments, log_totals, grad_heads
    )
    low_query = grad_query.astype(jnp.bfloat16)
    low_value = grad_value.astype(jnp.bfloat16)
    stacked = jnp.stack([low_query, grad_key.astype(jnp.bfloat16), low_value], axis=0)
    grad_packed = jnp.transpose(stacked, (2, 1, 0, 3)).reshape(tok_rows, 3 * heads_here * HD)
    qv_bias_grad = jnp.stack(
        [
            jnp.sum(low_query.astype(jnp.float32), axis=1),
            jnp.sum(low_value.astype(jnp.float32), axis=1),
        ],
        axis=1,
    ).reshape(-1)
    grad_qkv = jnp.einsum("rd,rc->dc", act_one, grad_packed, preferred_element_type=jnp.float32)
    grad_act_one = lax.psum_scatter(
        jnp.einsum("rc,dc->rd", grad_packed, qkv_full, preferred_element_type=jnp.float32).astype(
            jnp.bfloat16
        ),
        "narrow",
        scatter_dimension=1,
        tiled=True,
    ).astype(jnp.float32)
    hat_local = own_columns(hat_one, col_start, local_width)
    scaled = grad_act_one * first_gain.astype(jnp.float32)
    sum_plain, sum_hat = lax.psum(
        (jnp.sum(scaled, axis=1), jnp.sum(scaled * hat_local, axis=1)), "narrow"
    )
    full_width = local_width * lax.axis_size("narrow")
    grad_norm_one = inv_one * (
        scaled - sum_plain[:, None] / full_width - hat_local * sum_hat[:, None] / full_width
    )
    token_grad = (own_columns(grad_residual, col_start, local_width) + grad_norm_one).astype(
        jnp.bfloat16
    )
    first_gain_grad = jnp.sum(grad_act_one * hat_local, axis=0)
    first_shift_grad = jnp.sum(grad_act_one, axis=0)
    qkv_weight_grad, dense_weight_grad, up_weight_grad, down_weight_grad = (
        lax.psum_scatter(grad_qkv, "wide", scatter_dimension=0, tiled=True),
        lax.psum_scatter(grad_dense, "wide", scatter_dimension=1, tiled=True),
        lax.psum_scatter(grad_up, "wide", scatter_dimension=0, tiled=True),
        lax.psum_scatter(grad_down, "wide", scatter_dimension=1, tiled=True),
    )
    (
        first_gain_grad,
        first_shift_grad,
        qv_bias_grad,
        dense_bias_grad,
        second_gain_grad,
        second_shift_grad,
        up_bias_grad,
        down_bias_grad,
    ) = lax.psum(
        (
            first_gain_grad,
            first_shift_grad,
            qv_bias_grad,
            dense_bias_grad,
            second_gain_grad,
            second_shift_grad,
            up_bias_grad,
            down_bias_grad,
        ),
        "wide",
    )
    return (
        output,
        token_grad,
        first_gain_grad,
        first_shift_grad,
        qkv_weight_grad,
        qv_bias_grad,
        dense_weight_grad,
        dense_bias_grad,
        second_gain_grad,
        second_shift_grad,
        up_weight_grad,
        up_bias_grad,
        down_weight_grad,
        down_bias_grad,
    )


def solution(mesh):
    in_specs = (
        P("wide", "narrow"),
        P("wide"),
        P("narrow"),
        P("narrow"),
        P("wide", "narrow"),
        P("narrow"),
        P("narrow", "wide"),
        P("narrow"),
        P("narrow"),
        P("narrow"),
        P("wide", "narrow"),
        P("narrow"),
        P("narrow", "wide"),
        P("narrow"),
        P("wide", "narrow"),
    )
    out_specs = (
        P("wide", "narrow"),
        P("wide", "narrow"),
        P("narrow"),
        P("narrow"),
        P("wide", "narrow"),
        P("narrow"),
        P("narrow", "wide"),
        P("narrow"),
        P("narrow"),
        P("narrow"),
        P("wide", "narrow"),
        P("narrow"),
        P("narrow", "wide"),
        P("narrow"),
    )
    return jax.shard_map(local, mesh=mesh, in_specs=in_specs, out_specs=out_specs, check_vma=False)
```

profile of v0, /device:TPU:0, one launch (start us, length us, event | category | flops | bytes accessed | tf_op | source)
XLA Modules:
  0.0 781.6 jit_solution(9703250038963111462)
XLA Ops:
  10.8 12.6 %all-gather = bf16[4,1,256]{2,1,0:T(2,128)(2,1)S(1)} all-gather(bf16[1,1,256]{2,1,0:T(2,128)(2,1)S(1)} %reshape.217), channel_id=1, replica_groups=mesh['wide'=8,'narrow'=4] {'narrow'}, dimensions={0}, use_global_device_ids=true | all-gather | bytes 2560 | tf_op jit(solution)/shard_map/all_gather | solution.py:159
  32.0 11.9 %all_gather.37 = bf16[256,1024]{1,0:T(8,128)(2,1)} all-gather(bf16[256,128]{1,0:T(8,128)(2,1)} %param.29), channel_id=1, replica_groups=mesh['wide'=8,'narrow'=4] {'wide'}, dimensions={1}, use_global_device_ids=true | all-gather | bytes 589824 | tf_op jit(solution)/shard_map/all_gather | solution.py:167
  43.9 14.8 %all-gather.11.cloned.1.call-done = bf16[1024,1024]{1,0:T(8,128)(2,1)} async-done(((bf16[1024,256]{1,0:T(8,128)(2,1)}), bf16[1024,1024]{1,0:T(8,128)(2,1)}) %all-gather.11.cloned.1.call-update) | async-done | bytes 2097168 | tf_op jit(solution)/shard_map/all_gather | solution.py:158
  63.0 21.5 %all-gather.13.cloned.1.call-done = bf16[1024,768]{1,0:T(8,128)(2,1)} async-done(((bf16[128,768]{1,0:T(8,128)(2,1)}), bf16[1024,768]{1,0:T(8,128)(2,1)}) %all-gather.13.cloned.1.call-update) | async-done | bytes 1572880 | tf_op jit(solution)/shard_map/all_gather | solution.py:166
  100.6 13.1 %while.60 = (s32[]{:T(128)}, bf16[4,512,64]{1,2,0:T(8,128)(2,1)S(1)}, f32[4,512]{1,0:T(4,128)S(1)}, s32[1024]{0:T(1024)S(1)}, s32[1024]{0:T(1024)S(1)}, /*index=...) while((s32[]{:T(128)}, ...), condition=%wide.region_5.6_spmd.clone.clone, body=%wide.region_2.5_spmd.clone.sunk.clone | while | flops 70778368 | bytes 3707509 | solution.py:74
  113.7 20.1 %while.61 = (s32[]{:T(128)}, bf16[4,512,64]{1,2,0:T(8,128)(2,1)}, f32[4,512]{1,0:T(4,128)S(1)}, s32[1024]{0:T(1024)S(1)}, s32[1024]{0:T(1024)S(1)}, /*index=5*/b...) while((s32[]{:T(128)}, bf16[4,512,64]{1,2,0:T(8,128)(2,1)}, ...), condition=%wide.region_9.10_spmd.clone.clone, body=%wide.region_6.9_spmd.clone.sunk.clone | while | flops 141557248 | bytes 9217209 | solution.py:74
  140.7 10.9 %all-gather.4 = bf16[4,1,256]{2,1,0:T(2,128)(2,1)S(1)} all-gather(bf16[1,1,256]{2,1,0:T(2,128)(2,1)S(1)} %reshape.225), channel_id=1, replica_groups=mesh['wide'=8,'narrow'=4] {'narrow'}, dimensions={0}, use_global_device_ids=true | all-gather | bytes 2560 | tf_op jit(solution)/shard_map/all_gather | solution.py:163
  151.6 7.7 all-gather.3
  159.3 10.5 %all-gather.2 = bf16[4,1,256]{2,1,0:T(2,128)(2,1)S(1)} all-gather(bf16[1,1,256]{2,1,0:T(2,128)(2,1)S(1)} %reshape.221), channel_id=1, replica_groups=mesh['wide'=8,'narrow'=4] {'narrow'}, dimensions={0}, use_global_device_ids=true | all-gather | bytes 2560 | tf_op jit(solution)/shard_map/all_gather | solution.py:161
  169.8 55.9 %all-reduce.7.cloned.1.call-done = bf16[1024,1024]{1,0:T(8,128)(2,1)} async-done(((bf16[1024,1024]{1,0:T(8,128)(2,1)}), bf16[1024,1024]{1,0:T(8,128)(2,1)}) %all-reduce.7.cloned.1.call-update) | async-done | bytes 2097168 | tf_op jit(solution)/shard_map/psum | solution.py:194
  232.3 22.2 %all-gather.15.cloned.1.call-done = bf16[1024,1024]{1,0:T(8,128)(2,1)} async-done(((bf16[128,1024]{1,0:T(8,128)(2,1)}), bf16[1024,1024]{1,0:T(8,128)(2,1)}) %all-gather.15.cloned.1.call-update) | async-done | bytes 2097168 | tf_op jit(solution)/shard_map/all_gather | solution.py:170
  261.7 40.5 %all-gather.19.cloned.1.call-done = bf16[1024,1024]{1,0:T(8,128)(2,1)} async-done(((bf16[1024,256]{1,0:T(8,128)(2,1)}), bf16[1024,1024]{1,0:T(8,128)(2,1)}) %all-gather.19.cloned.1.call-update) | async-done | bytes 2097168 | tf_op jit(solution)/shard_map/all_gather | solution.py:216
  302.3 28.3 %all-gather.17.cloned.1.call-done = bf16[1024,1024]{1,0:T(8,128)(2,1)} async-done(((bf16[1024,128]{1,0:T(8,128)(2,1)}), bf16[1024,1024]{1,0:T(8,128)(2,1)}) %all-gather.17.cloned.1.call-update) | async-done | bytes 2097168 | tf_op jit(solution)/shard_map/all_gather | solution.py:171
  330.6 8.4 %convert_reduce_fusion.2 = (f32[1024]{0:T(1024)S(1)}, bf16[1024,1024]{1,0:T(8,128)(2,1)S(1)}) fusion(f32[1024,1024]{1,0:T(8,128)} %fusion.85, f32[1024]{0:T(1024)S(1)} %convert_element_type.169, bf16[1024,1024]{1,0:T(8,128)(2,1)} %all-gather.19.cloned.1.call-done, bf16[1024,1024]{1,0:T(8,128)(2,1)} %all-gather.17.cloned.1.call-done), kind=kOutput, calls=%fused_computation.108 | convolution fusion | flops 2171599872 | bytes 10493952 | tf_op jit(solution)/shard_map/rd,fd->rf/dot_general | solution.py:219
  352.2 78.5 %all-reduce.9.cloned.1.call-done = bf16[1024,1024]{1,0:T(8,128)(2,1)} async-done(((bf16[1024,1024]{1,0:T(8,128)(2,1)}), bf16[1024,1024]{1,0:T(8,128)(2,1)}) %all-reduce.9.cloned.1.call-update) | async-done | bytes 2097168 | tf_op jit(solution)/shard_map/psum | solution.py:224
  444.5 42.0 %while.63 = (s32[]{:T(128)}, bf16[4,512,64]{1,2,0:T(8,128)(2,1)S(1)}, f32[4,1024,64]{1,2,0:T(8,128)}, f32[4,1024,64]{1,2,0:T(8,128)}, s32[1024]{0:T(1024)S(1)}, ...) while((s32[]{:T(128)}, ...), condition=%wide.region_22.23_spmd.clone.clone, body=%wide.region_20.22_spmd.clone.sunk.clone | while | flops 344030720 | bytes 17733272 | solution.py:124
  486.5 37.5 %while.62 = (s32[]{:T(128)}, bf16[4,512,64]{1,2,0:T(8,128)(2,1)}, f32[4,512,64]{1,2,0:T(8,128)}, f32[4,512,64]{1,2,0:T(8,128)}, s32[1024]{0:T(1024)S(1)}, /*inde...) while((s32[]{:T(128)}, bf16[4,512,64]{1,2,0:T(8,128)(2,1)}, ...), condition=%wide.region_19.20_spmd.clone.clone, body=%wide.region_17.19_spmd.clone.sunk.clone | while | flops 172031488 | bytes 11304645 | solution.py:124
  535.9 8.1 %fusion.83 = f32[1024,1024]{1,0:T(8,128)} fusion(bf16[1024,1024]{1,0:T(8,128)(2,1)} %all-gather.19.cloned.1.call-done, f32[1024,1024]{1,0:T(8,128)} %fusion.85, f32[1024]{0:T(1024)S(1)} %convert_element_type.169), kind=kOutput, calls=%fused_computation.163 | convolution fusion | flops 2157969408 | bytes 10489856 | tf_op jit(solution)/shard_map/rf,rd->fd/dot_general | solution.py:217
  560.1 14.5 %reduce-scatter.9.cloned.1.call-done = bf16[1024,256]{1,0:T(8,128)(2,1)} async-done(((bf16[1024,1024]{1,0:T(8,128)(2,1)}), bf16[1024,256]{1,0:T(8,128)(2,1)}) %reduce-scatter.9.cloned.1.call-update) | async-done | bytes 524304 | tf_op jit(solution)/shard_map/reduce_scatter | solution.py:260
  576.5 23.9 %all-reduce.2 = (f32[256]{0:T(256)}, f32[256]{0:T(256)}, f32[512]{0:T(512)}, f32[256]{0:T(256)}, f32[256]{0:T(256)}, /*index=5*/f32[256]{0:T(256)}, f32[1024]{0:T(1024)}, f32[256]{0:T(256)}) all-reduce(f32[256]{0:T(256)S(1)} %get-tuple-element.362, f32[256]{0:T(256)S(1)} %get-tuple-element.367, ...), channel_id=1, replica_groups=mesh['wide'=8,'narrow'=4] {'wide'}, use_global_device_ids=true, to_apply=%region_29.30 | all-reduce | flops 3072 | bytes 24576 | tf_op jit(solution)/shard_map/psum | solution.py:297
  600.4 10.3 %all-reduce.3 = (f32[1024]{0:T(1024)S(1)}, f32[1024]{0:T(1024)S(1)}) all-reduce(f32[1024]{0:T(1024)S(1)} %get-tuple-element.363, f32[1024]{0:T(1024)S(1)} %get-tuple-element.366), channel_id=1, replica_groups=mesh['wide'=8,'narrow'=4] {'narrow'}, use_global_device_ids=true, to_apply=%region_27.28 | all-reduce | flops 2048 | bytes 16384 | tf_op jit(solution)/shard_map/psum | solution.py:270
  613.7 55.2 %reduce-scatter.17.cloned.1.call-done = f32[1024,128]{1,0:T(8,128)} async-done(((f32[1024,1024]{1,0:T(8,128)}), f32[1024,128]{1,0:T(8,128)}) %reduce-scatter.17.cloned.1.call-update) | async-done | bytes 524304 | tf_op jit(solution)/shard_map/reduce_scatter | solution.py:286
  668.9 55.5 %reduce-scatter.15.cloned.1.call-done = f32[128,1024]{1,0:T(8,128)} async-done(((f32[1024,1024]{1,0:T(8,128)}), f32[128,1024]{1,0:T(8,128)}) %reduce-scatter.15.cloned.1.call-update) | async-done | bytes 524304 | tf_op jit(solution)/shard_map/reduce_scatter | solution.py:285
  724.4 50.2 %reduce-scatter.11.cloned.1.call-done = f32[128,768]{1,0:T(8,128)} async-done(((f32[1024,768]{1,0:T(8,128)}), f32[128,768]{1,0:T(8,128)}) %reduce-scatter.11.cloned.1.call-update) | async-done | bytes 393232 | tf_op jit(solution)/shard_map/reduce_scatter | solution.py:283
  (326 shorter events, 224.9 us)
Async XLA Ops:
  7.2 51.4 %all-gather.11.cloned.1.call-start = ((), (), s32[]{:S(2)}) async-start(), calls=%async_computation.6 | async-start | bytes 2621440 | tf_op jit(solution)/shard_map/all_gather | solution.py:158
  7.9 76.5 %all-gather.13.cloned.1.call-start = ((), (), s32[]{:S(2)}) async-start(), calls=%async_computation.7 | async-start | bytes 1769472 | tf_op jit(solution)/shard_map/all_gather | solution.py:166
  8.7 217.1 %all-reduce.7.cloned.1.call-start = ((), (), s32[]{:S(2)}) async-start(), calls=%async_computation.8 | async-start | bytes 4194304 | tf_op jit(solution)/shard_map/psum | solution.py:194
  8.7 81.0 %copy-start.4 = (bf16[4,512,64]{1,2,0:T(8,128)(2,1)}, bf16[4,512,64]{1,2,0:T(8,128)(2,1)S(1)}, u32[]{:S(2)}) copy-start(bf16[4,512,64]{1,2,0:T(8,128)(2,1)S(1)} %fusion.93) | copy-start | bytes 786436
  58.6 25.8 %copy-start.3 = (bf16[1024,1024]{1,0:T(8,128)(2,1)S(1)}, bf16[1024,1024]{1,0:T(8,128)(2,1)}, u32[]{:S(2)}) copy-start(bf16[1024,1024]{1,0:T(8,128)(2,1)} %all-gather.11.cloned.1.call-done) | copy-start | bytes 6291460
  133.8 6.8 copy-start.22
  133.9 6.8 copy-start.23
  133.9 6.8 copy-start.24
  133.9 35.9 %copy-start.19 = (bf16[1024]{0:T(1024)(128)(2,1)S(1)}, bf16[1024]{0:T(1024)(128)(2,1)}, u32[]{:S(2)}) copy-start(bf16[1024]{0:T(1024)(128)(2,1)} %param.34) | copy-start | bytes 6148
  138.8 115.7 %all-gather.15.cloned.1.call-start = ((), (), s32[]{:S(2)}) async-start(), calls=%async_computation.9 | async-start | bytes 2359296 | tf_op jit(solution)/shard_map/all_gather | solution.py:170
  139.4 162.9 %all-gather.19.cloned.1.call-start = ((), (), s32[]{:S(2)}) async-start(), calls=%async_computation.12 | async-start | bytes 2621440 | tf_op jit(solution)/shard_map/all_gather | solution.py:216
  140.0 190.6 %all-gather.17.cloned.1.call-start = ((), (), s32[]{:S(2)}) async-start(), calls=%async_computation.10 | async-start | bytes 2359296 | tf_op jit(solution)/shard_map/all_gather | solution.py:171
  140.6 290.2 %all-reduce.9.cloned.1.call-start = ((), (), s32[]{:S(2)}) async-start(), calls=%async_computation.13 | async-start | bytes 4194304 | tf_op jit(solution)/shard_map/psum | solution.py:224
  330.6 9.7 %copy-start.20 = (bf16[1024,1024]{1,0:T(8,128)(2,1)S(1)}, bf16[1024,1024]{1,0:T(8,128)(2,1)}, u32[]{:S(2)}) copy-start(bf16[1024,1024]{1,0:T(8,128)(2,1)} %all-gather.15.cloned.1.call-done) | copy-start | bytes 6291460
  344.1 213.7 %reduce-scatter.7.cloned.1.call-start = ((), (), s32[]{:S(2)}) async-start(), calls=%async_computation.11 | async-start | bytes 2621440 | tf_op jit(solution)/shard_map/reduce_scatter | solution.py:207
  352.2 222.4 %reduce-scatter.9.cloned.1.call-start = ((), (), s32[]{:S(2)}) async-start(), calls=%async_computation.14 | async-start | bytes 2621440 | tf_op jit(solution)/shard_map/reduce_scatter | solution.py:260
  487.1 5.6 copy-start.11
  496.5 5.7 copy-start.11
  505.9 5.7 copy-start.11
  515.2 5.7 copy-start.11
  531.6 82.0 %reduce-scatter.13.cloned.1.call-start = ((), (), s32[]{:S(2)}) async-start(), calls=%async_computation.16 | async-start | bytes 1179648 | tf_op jit(solution)/shard_map/reduce_scatter | solution.py:284
  535.9 133.0 %reduce-scatter.17.cloned.1.call-start = ((), (), s32[]{:S(2)}) async-start(), calls=%async_computation.18 | async-start | bytes 4718592 | tf_op jit(solution)/shard_map/reduce_scatter | solution.py:286
  544.1 180.4 %reduce-scatter.15.cloned.1.call-start = ((), (), s32[]{:S(2)}) async-start(), calls=%async_computation.17 | async-start | bytes 4718592 | tf_op jit(solution)/shard_map/reduce_scatter | solution.py:285
  551.7 223.0 %reduce-scatter.11.cloned.1.call-start = ((), (), s32[]{:S(2)}) async-start(), calls=%async_computation.15 | async-start | bytes 3538944 | tf_op jit(solution)/shard_map/reduce_scatter | solution.py:283
  (29 other events, 82.1 us)
Sparse Core Ops, SparseCore 0:
  9.6 48.9 all-gather.10
  60.5 23.9 all-gather.12
  138.9 86.7 all-reduce.6
  227.6 26.8 all-gather.14
  256.0 46.2 all-gather.18
  304.1 26.4 all-gather.16
  344.2 86.5 all-reduce.8
  433.0 42.8 reduce-scatter.6
  531.8 42.8 reduce-scatter.8
  578.2 35.3 reduce-scatter.12
  617.6 51.2 reduce-scatter.16
  673.0 51.3 reduce-scatter.14
  728.4 46.2 reduce-scatter.10
where the time goes:
time: 790 us; the launch traced here: 782 us
  waiting for transfers between devices  440 us (56%)
  matrix products  159 us (20%)
  blocking collectives  95.4 us (12%)
  other arithmetic  36.9 us (5%)
  local copies, waits for them, and re-layouts  34.1 us (4%)
  between operations  14.8 us (2%)
    psum x1, waiting for transfers between devices, local(): lax.psum(jnp.einsum('rf,df->rd', grad_pre, up_full, preferred_element_typ...  78.5 us
    psum x1, waiting for transfers between devices, local(): lax.psum(jnp.dot(attended, dense_full, preferred_element_type=jnp.float32...  55.9 us
    reduce_scatter x1, waiting for transfers between devices, local(): lax.psum_scatter(grad_up, 'wide', scatter_dimension=0, tiled=True)  55.5 us
    reduce_scatter x1, waiting for transfers between devices, local(): lax.psum_scatter(grad_down, 'wide', scatter_dimension=1, tiled=True)  55.2 us
    reduce_scatter x1, waiting for transfers between devices, local(): lax.psum_scatter(grad_qkv, 'wide', scatter_dimension=0, tiled=True)  50.2 us
    all_gather x1, waiting for transfers between devices, local(): grad_out = lax.all_gather(cotangent, 'narrow', axis=1, tiled=True)  40.5 us
    dot_general x16, matrix products, masked_scores(): jnp.einsum('qd,kd->qk', query_block, key_block, preferred_element_type=jn...  39.3 us
    all_gather x1, waiting for transfers between devices, local(): lax.all_gather(down_weight, 'wide', axis=1, tiled=True)  28.3 us
  transfers between devices with their start and end apart: 13, of which 11 were waited for; matrix products, arithmetic and copies ran while one was open for 20% of the time, Pallas kernels for 0%

commit v1 on v0

v1 whole, which is shorter than its diff:
```python
from functools import partial

import jax
import jax.numpy as jnp
from jax import lax
from jax.experimental import pallas as pl
from jax.experimental.pallas import tpu as pltpu
from jax.sharding import PartitionSpec as P

H = 16
HD = 64


eps = 1e-05
negative = -1e30
block_rows = 256
head_group = 2


def normalize(values, gain, shift):
    mean_value = jnp.mean(values, axis=-1, keepdims=True)
    centered = values - mean_value
    inv_std = lax.rsqrt(jnp.mean(centered * centered, axis=-1, keepdims=True) + eps)
    normed = centered * inv_std
    return (normed * gain + shift, normed, inv_std)


def norm_backward(grad_norm, gain, normed, inv_std):
    scaled = grad_norm * gain
    mean_one = jnp.mean(scaled, axis=-1, keepdims=True)
    mean_two = jnp.mean(scaled * normed, axis=-1, keepdims=True)
    return inv_std * (scaled - mean_one - normed * mean_two)


def own_columns(values, col_start, local_width):
    return lax.dynamic_slice_in_dim(values, col_start, local_width, values.ndim - 1)


def contract(left, right, left_dim, right_dim):
    return lax.dot_general(
        left, right, (((left_dim,), (right_dim,)), ((), ())), preferred_element_type=jnp.float32
    )


def score_block(seg_ref, query_block, keys, slope, row_start, tok_rows):
    row_end = keys.shape[0]
    logits = contract(keys, query_block, 1, 1)
    key_pos = lax.broadcasted_iota(jnp.int32, (row_end, 1), 0)
    query_pos = row_start + lax.broadcasted_iota(jnp.int32, (1, query_block.shape[0]), 1)
    half = tok_rows // 2
    shared = (seg_ref[0] == seg_ref[half]).astype(jnp.int32)
    first_key = 0 if row_start < half else jnp.where(shared == 1, 0, half)
    key_term = slope * (key_pos - row_start).astype(jnp.float32)
    allowed = (key_pos <= query_pos) & (key_pos >= first_key)
    return jnp.where(allowed, logits + key_term, negative)


def forward_body(seg_ref, slope_ref, packed_ref, out_ref, total_ref):
    tok_rows = packed_ref.shape[0]
    group = pl.program_id(0)
    for item in range(head_group):
        slope = slope_ref[group * head_group + item]
        base = item * 3 * HD
        for row_start in range(0, tok_rows, block_rows):
            row_end = row_start + block_rows
            rows = slice(row_start, row_end)
            query = packed_ref[rows, base : base + HD] * jnp.bfloat16(HD ** (-0.5))
            keys = packed_ref[:row_end, base + HD : base + 2 * HD]
            values = packed_ref[:row_end, base + 2 * HD : base + 3 * HD]
            logits = score_block(seg_ref, query, keys, slope, row_start, tok_rows)
            top = jnp.max(logits, axis=0, keepdims=True)
            powers = jnp.exp(logits - top)
            total = jnp.sum(powers, axis=0, keepdims=True)
            probs = (powers * (1.0 / total)).astype(jnp.bfloat16)
            result = contract(values, probs, 0, 0)
            out_ref[rows, item * HD : (item + 1) * HD] = result.T.astype(jnp.bfloat16)
            total_ref[0, item : item + 1, rows] = top + jnp.log(total)


def backward_body(seg_ref, slope_ref, packed_ref, total_ref, grad_ref, out_ref, key_sum, value_sum):
    tok_rows = packed_ref.shape[0]
    group = pl.program_id(0)
    scale = HD ** (-0.5)
    for item in range(head_group):
        slope = slope_ref[group * head_group + item]
        base = item * 3 * HD
        for row_start in reversed(range(0, tok_rows, block_rows)):
            row_end = row_start + block_rows
            rows = slice(row_start, row_end)
            query = packed_ref[rows, base : base + HD] * jnp.bfloat16(scale)
            keys = packed_ref[:row_end, base + HD : base + 2 * HD]
            values = packed_ref[:row_end, base + 2 * HD : base + 3 * HD]
            grad = grad_ref[rows, item * HD : (item + 1) * HD]
            logits = score_block(seg_ref, query, keys, slope, row_start, tok_rows)
            probs = jnp.exp(logits - total_ref[0, item : item + 1, rows])
            grad_probs = contract(values, grad, 1, 1)
            weighted = jnp.sum(probs * grad_probs, axis=0, keepdims=True)
            grad_logits = (probs * (grad_probs - weighted)).astype(jnp.bfloat16)
            grad_query = contract(keys, grad_logits, 0, 0) * scale
            out_ref[rows, base : base + HD] = grad_query.T.astype(jnp.bfloat16)
            grad_key = contract(grad_logits, query, 1, 0)
            grad_value = contract(probs.astype(jnp.bfloat16), grad, 1, 0)
            if row_end == tok_rows:
                key_sum[...] = grad_key
                value_sum[...] = grad_value
            else:
                key_sum[:row_end, :] += grad_key
                value_sum[:row_end, :] += grad_value
        out_ref[:, base + HD : base + 2 * HD] = key_sum[...].astype(jnp.bfloat16)
        out_ref[:, base + 2 * HD : base + 3 * HD] = value_sum[...].astype(jnp.bfloat16)


def attend_specs(tok_rows):
    scalars = pl.BlockSpec(memory_space=pltpu.SMEM)
    packed = pl.BlockSpec((tok_rows, head_group * 3 * HD), lambda g: (0, g))
    totals = pl.BlockSpec((1, head_group, tok_rows), lambda g: (g, 0, 0))
    heads = pl.BlockSpec((tok_rows, head_group * HD), lambda g: (0, g))
    return scalars, packed, totals, heads


def attend_forward(packed, slopes, segments):
    tok_rows, width = packed.shape
    heads_here = width // (3 * HD)
    groups = heads_here // head_group
    scalars, packed_spec, totals, heads = attend_specs(tok_rows)
    return pl.pallas_call(
        forward_body,
        grid=(groups,),
        in_specs=[scalars, scalars, packed_spec],
        out_specs=[heads, totals],
        out_shape=[
            jax.ShapeDtypeStruct((tok_rows, heads_here * HD), jnp.bfloat16),
            jax.ShapeDtypeStruct((groups, head_group, tok_rows), jnp.float32),
        ],
        compiler_params=pltpu.CompilerParams(vmem_limit_bytes=40 * 2**20),
        cost_estimate=pl.CostEstimate(
            flops=4 * heads_here * tok_rows * tok_rows * HD,
            bytes_accessed=2 * tok_rows * width * 2,
            transcendentals=heads_here * tok_rows * tok_rows,
        ),
    )(segments, slopes, packed)


def attend_backward(packed, slopes, segments, log_totals, grad_attended):
    tok_rows, width = packed.shape
    heads_here = width // (3 * HD)
    scalars, packed_spec, totals, heads = attend_specs(tok_rows)
    return pl.pallas_call(
        backward_body,
        grid=(heads_here // head_group,),
        in_specs=[scalars, scalars, packed_spec, totals, heads],
        out_specs=packed_spec,
        out_shape=jax.ShapeDtypeStruct((tok_rows, width), jnp.bfloat16),
        scratch_shapes=[
            pltpu.VMEM((tok_rows, HD), jnp.float32),
            pltpu.VMEM((tok_rows, HD), jnp.float32),
        ],
        compiler_params=pltpu.CompilerParams(vmem_limit_bytes=40 * 2**20),
        cost_estimate=pl.CostEstimate(
            flops=10 * heads_here * tok_rows * tok_rows * HD,
            bytes_accessed=3 * tok_rows * width * 2,
            transcendentals=heads_here * tok_rows * tok_rows,
        ),
    )(segments, slopes, packed, log_totals, grad_attended)


def exchange_body(scatter, count, devices, *refs):
    sources, results = refs[:count], refs[count : 2 * count]
    local_sem, send_sem, recv_sem = refs[2 * count :]
    me = lax.axis_index("wide")

    barrier = pltpu.get_barrier_semaphore()

    def greet(step, carry):
        peer = lax.rem(me + step, devices)
        pl.semaphore_signal(
            barrier, inc=1, device_id={"wide": peer}, device_id_type=pl.DeviceIdType.MESH
        )
        return carry

    lax.fori_loop(1, devices, greet, 0)
    pl.semaphore_wait(barrier, devices - 1)

    def block_of(item, owner):
        return sources[item].at[owner] if scatter else sources[item]

    def copy_to(item, step):
        peer = lax.rem(me + step, devices)
        return pltpu.make_async_remote_copy(
            src_ref=block_of(item, peer),
            dst_ref=results[item].at[me],
            send_sem=send_sem.at[item, step],
            recv_sem=recv_sem.at[item, step],
            device_id={"wide": peer},
            device_id_type=pl.DeviceIdType.MESH,
        )

    def own_copy(item):
        return pltpu.make_async_copy(
            block_of(item, me), results[item].at[me], local_sem.at[item]
        )

    def start(step, carry):
        for item in range(count):
            copy_to(item, step).start()
        return carry

    def finish(step, carry):
        for item in range(count):
            copy_to(item, step).wait()
        return carry

    lax.fori_loop(1, devices, start, 0)
    for item in range(count):
        own_copy(item).start()
    for item in range(count):
        own_copy(item).wait()
    lax.fori_loop(1, devices, finish, 0)


def exchange(sources, scatter, call_id):
    devices = lax.axis_size("wide")
    count = len(sources)
    shapes = [item.shape[1:] if scatter else item.shape for item in sources]
    size = sum(devices * rows * width * 2 for rows, width in shapes)
    return pl.pallas_call(
        partial(exchange_body, scatter, count, devices),
        in_specs=[pl.BlockSpec(memory_space=pl.ANY)] * count,
        out_specs=[pl.BlockSpec(memory_space=pl.ANY)] * count,
        out_shape=[
            jax.ShapeDtypeStruct((devices, *shape), item.dtype)
            for shape, item in zip(shapes, sources)
        ],
        scratch_shapes=[
            pltpu.SemaphoreType.DMA((count,)),
            pltpu.SemaphoreType.DMA((count, devices)),
            pltpu.SemaphoreType.DMA((count, devices)),
        ],
        compiler_params=pltpu.CompilerParams(collective_id=call_id, has_side_effects=True),
        cost_estimate=pl.CostEstimate(flops=0, bytes_accessed=20 * size, transcendentals=0),
    )(*sources)


def gather_rows(sources, call_id):
    return [
        item.reshape(-1, item.shape[-1]) for item in exchange(sources, False, call_id)
    ]


def scatter_sums(sources, call_id):
    devices = lax.axis_size("wide")
    blocks = [item.reshape(devices, -1, item.shape[-1]) for item in sources]
    return [
        jnp.sum(item.astype(jnp.float32), axis=0) for item in exchange(blocks, True, call_id)
    ]


def local(
    tokens,
    segments,
    first_gain,
    first_shift,
    qkv_weight,
    qv_bias,
    dense_weight,
    dense_bias,
    second_gain,
    second_shift,
    up_weight,
    up_bias,
    down_weight,
    down_bias,
    cotangent,
):
    tok_rows, local_width = tokens.shape
    col_start = lax.axis_index("narrow") * local_width
    heads_here = qv_bias.shape[0] // (2 * HD)
    head_first = lax.axis_index("narrow") * heads_here
    slopes = 2.0 ** (-8.0 * (head_first + jnp.arange(heads_here) + 1).astype(jnp.float32) / H)
    out_rows = dense_weight.shape[1]
    vectors = jnp.stack([first_gain, first_shift, dense_bias, second_gain, second_shift])
    vectors = jnp.pad(vectors, ((0, 11), (0, 0)))
    joined = lax.all_gather(
        jnp.concatenate([tokens, dense_weight.T, vectors], axis=0), "narrow", axis=1, tiled=True
    )
    full_tokens = joined[:tok_rows]
    dense_block = joined[tok_rows : tok_rows + out_rows]
    gain_one, shift_one, bias_dense, gain_two, shift_two = (
        joined[tok_rows + out_rows + item].astype(jnp.float32) for item in range(5)
    )
    qkv_full, up_full = gather_rows([qkv_weight, up_weight], 0)
    grad_out = lax.all_gather(cotangent, "narrow", axis=1, tiled=True)
    inputs = full_tokens.astype(jnp.float32)
    normed_one, hat_one, inv_one = normalize(inputs, gain_one, shift_one)
    act_one = normed_one.astype(jnp.bfloat16)
    bias_pair = qv_bias.astype(jnp.float32).reshape(heads_here, 2, HD)
    full_bias = jnp.stack(
        [bias_pair[:, 0], jnp.zeros_like(bias_pair[:, 0]), bias_pair[:, 1]], axis=1
    ).reshape(-1)
    packed = (
        jnp.dot(act_one, qkv_full, preferred_element_type=jnp.float32) + full_bias[None]
    ).astype(jnp.bfloat16)
    attended, log_totals = attend_forward(packed, slopes, segments)
    attended_full = lax.all_gather(attended, "narrow", axis=1, tiled=True)
    dense_rows, down_rows = gather_rows([dense_block, down_weight.T], 1)
    mixed = contract(attended_full, dense_rows, 1, 1)
    residual = inputs + (mixed + bias_dense)
    normed_two, hat_two, inv_two = normalize(residual, gain_two, shift_two)
    act_two = normed_two.astype(jnp.bfloat16)
    pre_act = jnp.dot(act_two, up_full, preferred_element_type=jnp.float32) + up_bias.astype(
        jnp.float32
    )
    hidden = jax.nn.gelu(pre_act, approximate=True).astype(jnp.bfloat16)
    grad_hidden = jnp.dot(grad_out, down_rows, preferred_element_type=jnp.float32)
    _, gelu_back = jax.vjp(partial(jax.nn.gelu, approximate=True), pre_act)
    grad_pre = gelu_back(grad_hidden)[0].astype(jnp.bfloat16)
    grad_act_two = lax.psum(
        contract(grad_pre, up_full, 1, 1).astype(jnp.bfloat16), "narrow"
    ).astype(jnp.float32)
    mlp_out = lax.psum_scatter(
        contract(hidden, down_rows, 1, 1).astype(jnp.bfloat16),
        "narrow",
        scatter_dimension=1,
        tiled=True,
    ).astype(jnp.float32)
    output = (
        own_columns(residual, col_start, local_width) + (mlp_out + down_bias.astype(jnp.float32))
    ).astype(jnp.bfloat16)
    down_bias_grad = jnp.sum(cotangent.astype(jnp.float32), axis=0)
    up_bias_grad = jnp.sum(grad_pre.astype(jnp.float32), axis=0)
    grad_down = contract(grad_out, hidden, 0, 0).astype(jnp.bfloat16)
    grad_up = contract(act_two, grad_pre, 0, 0).astype(jnp.bfloat16)
    up_weight_grad, down_rows_grad = scatter_sums([grad_up, grad_down], 2)
    second_gain_grad = own_columns(jnp.sum(grad_act_two * hat_two, axis=0), col_start, local_width)
    second_shift_grad = own_columns(jnp.sum(grad_act_two, axis=0), col_start, local_width)
    grad_residual = grad_out.astype(jnp.float32) + norm_backward(
        grad_act_two, gain_two, hat_two, inv_two
    )
    grad_branch = grad_residual.astype(jnp.bfloat16)
    dense_bias_grad = own_columns(
        jnp.sum(grad_branch.astype(jnp.float32), axis=0), col_start, local_width
    )
    grad_attended = jnp.dot(
        grad_branch,
        own_columns(dense_rows, col_start, local_width),
        preferred_element_type=jnp.float32,
    ).astype(jnp.bfloat16)
    grad_packed = attend_backward(packed, slopes, segments, log_totals, grad_attended)
    column_sums = jnp.sum(grad_packed.astype(jnp.float32), axis=0).reshape(heads_here, 3, HD)
    qv_bias_grad = jnp.stack([column_sums[:, 0], column_sums[:, 2]], axis=1).reshape(-1)
    grad_one_part = contract(grad_packed, qkv_full, 1, 1)
    grad_act_one = lax.psum_scatter(
        grad_one_part.astype(jnp.bfloat16), "narrow", scatter_dimension=1, tiled=True
    ).astype(jnp.float32)
    scaled_part = grad_one_part * gain_one
    sum_plain, sum_hat, gain_part, shift_part = lax.psum(
        (
            jnp.sum(scaled_part, axis=1),
            jnp.sum(scaled_part * hat_one, axis=1),
            jnp.sum(grad_one_part * hat_one, axis=0),
            jnp.sum(grad_one_part, axis=0),
        ),
        "narrow",
    )
    grad_qkv = contract(act_one, grad_packed, 0, 0).astype(jnp.bfloat16)
    grad_dense = contract(grad_branch, attended, 0, 0).astype(jnp.bfloat16)
    qkv_weight_grad, dense_rows_grad = scatter_sums([grad_qkv, grad_dense], 3)
    small = (
        own_columns(gain_part, col_start, local_width),
        own_columns(shift_part, col_start, local_width),
        qv_bias_grad,
        dense_bias_grad,
        second_gain_grad,
        second_shift_grad,
        up_bias_grad,
        down_bias_grad,
    )
    small_sums = lax.psum(jnp.concatenate(small), "wide")
    bounds = [0]
    for item in small:
        bounds.append(bounds[-1] + item.shape[0])
    (
        first_gain_grad,
        first_shift_grad,
        qv_bias_grad,
        dense_bias_grad,
        second_gain_grad,
        second_shift_grad,
        up_bias_grad,
        down_bias_grad,
    ) = (small_sums[low:high] for low, high in zip(bounds, bounds[1:]))
    hat_local = own_columns(hat_one, col_start, local_width)
    scaled = grad_act_one * first_gain.astype(jnp.float32)
    full_width = local_width * lax.axis_size("narrow")
    grad_norm_one = inv_one * (
        scaled - sum_plain[:, None] / full_width - hat_local * sum_hat[:, None] / full_width
    )
    token_grad = (own_columns(grad_residual, col_start, local_width) + grad_norm_one).astype(
        jnp.bfloat16
    )
    dense_weight_grad = dense_rows_grad.T
    down_weight_grad = down_rows_grad.T
    return (
        output,
        token_grad,
        first_gain_grad,
        first_shift_grad,
        qkv_weight_grad,
        qv_bias_grad,
        dense_weight_grad,
        dense_bias_grad,
        second_gain_grad,
        second_shift_grad,
        up_weight_grad,
        up_bias_grad,
        down_weight_grad,
        down_bias_grad,
    )


def solution(mesh):
    in_specs = (
        P("wide", "narrow"),
        P("wide"),
        P("narrow"),
        P("narrow"),
        P("wide", "narrow"),
        P("narrow"),
        P("narrow", "wide"),
        P("narrow"),
        P("narrow"),
        P("narrow"),
        P("wide", "narrow"),
        P("narrow"),
        P("narrow", "wide"),
        P("narrow"),
        P("wide", "narrow"),
    )
    out_specs = (
        P("wide", "narrow"),
        P("wide", "narrow"),
        P("narrow"),
        P("narrow"),
        P("wide", "narrow"),
        P("narrow"),
        P("narrow", "wide"),
        P("narrow"),
        P("narrow"),
        P("narrow"),
        P("wide", "narrow"),
        P("narrow"),
        P("narrow", "wide"),
        P("narrow"),
    )
    return jax.shard_map(local, mesh=mesh, in_specs=in_specs, out_specs=out_specs, check_vma=False)
```

time: 790 us -> 460 us (0.58)
  waiting for transfers between devices: 440 us -> 105 us
  Pallas kernels: 0 us -> 189 us
  matrix products: 159 us -> 59.3 us
  blocking collectives: 95.4 us -> 39 us
  local copies, waits for them, and re-layouts: 34.1 us -> 15.9 us
  other arithmetic: 36.9 us -> 28.5 us
    pallas_call x0 -> x6, Pallas kernels: none -> 189 us  [the longest x4 166 us: exchange(): pl.pallas_call(partial(exchange_body, scatter, count, devices), in_specs=...]
    reduce_scatter x6 -> x2, waiting for transfers between devices: 175 us -> 0.01 us  [the longest x1 0.01 us: local(): lax.psum_scatter(contract(hidden, down_rows, 1, 1).astype(jnp.bfloat16),...]
    dot_general x66 -> x10, matrix products: 146 us -> 52.8 us  [the longest x8 42.2 us: contract(): lax.dot_general(left, right, (((left_dim,), (right_dim,)), ((), ())), pre...]
    all_gather x4 -> x2, waiting for transfers between devices: 86.8 us -> 8.49 us  [the longest x1 8.47 us: local(): lax.all_gather(jnp.concatenate([tokens, dense_weight.T, vectors], axis=0)...]
    psum x2 -> x1, waiting for transfers between devices: 134 us -> 70.4 us  [local(): lax.psum(contract(grad_pre, up_full, 1, 1).astype(jnp.bfloat16), 'narrow')]
    all_gather x6 -> x0, blocking collectives: 61.2 us -> none  [the longest x1 12.6 us: local(): lax.all_gather(first_gain, 'narrow', axis=0, tiled=True)]
    all_gather x1, waiting for transfers between devices: 40.5 us -> 25.6 us  [local(): grad_out = lax.all_gather(cotangent, 'narrow', axis=1, tiled=True)]
    dynamic_slice x19 -> x0, local copies, waits for them, and re-layouts: 9.58 us -> none  [the longest x16 9.35 us: attend_forward(): head_out, head_total = lax.map(one_head, (query, keys, values, slopes))]
  transfers between devices with their start and end apart: 13 -> 6, of which waited for: 11 -> 3; matrix products, arithmetic and copies ran while one was open for 20% -> 16% of each run, Pallas kernels for 0% -> 39%
where the time goes in v1:
time: 460 us; the launch traced here: 453 us
  Pallas kernels  189 us (41%)
  waiting for transfers between devices  105 us (23%)
  matrix products  59.3 us (13%)
  blocking collectives  39 us (8%)
  other arithmetic  28.5 us (6%)
  local copies, waits for them, and re-layouts  15.9 us (3%)
  between operations  15 us (3%)
    pallas_call x4, Pallas kernels, exchange(): pl.pallas_call(partial(exchange_body, scatter, count, devices), in_specs=...  166 us
    psum x1, waiting for transfers between devices, local(): lax.psum(contract(grad_pre, up_full, 1, 1).astype(jnp.bfloat16), 'narrow')  70.4 us
    dot_general x8, matrix products, contract(): lax.dot_general(left, right, (((left_dim,), (right_dim,)), ((), ())), pre...  42.2 us
    all_gather x1, waiting for transfers between devices, local(): grad_out = lax.all_gather(cotangent, 'narrow', axis=1, tiled=True)  25.6 us
    psum x1, blocking collectives, local(): small_sums = lax.psum(jnp.concatenate(small), 'wide')  22.3 us
    psum x1, blocking collectives, local(): lax.psum((jnp.sum(scaled_part, axis=1), jnp.sum(scaled_part * hat_one, ax...  16.7 us
    pallas_call x1, Pallas kernels, attend_backward(): pl.pallas_call(backward_body, grid=(heads_here // head_group,), in_specs=...  12.8 us
    pallas_call x1, Pallas kernels, attend_forward(): pl.pallas_call(forward_body, grid=(groups,), in_specs=[scalars, scalars,...  10.8 us
  transfers between devices with their start and end apart: 6, of which 3 were waited for; matrix products, arithmetic and copies ran while one was open for 16% of the time, Pallas kernels for 39%

profile of v1, /device:TPU:0, one launch (start us, length us, event | category | flops | bytes accessed | tf_op | source)
XLA Modules:
  0.0 453.0 jit_solution(491294310268941991)
XLA Ops:
  14.5 44.4 %shard_map.254 = (bf16[8,128,768]{2,1,0:T(8,128)(2,1)}, bf16[8,128,1024]{2,1,0:T(8,128)(2,1)}) custom-call(bf16[128,768]{1,0:T(8,128)(2,1)} %refs_0_.1, bf16[128,1024]{1,0:T(8,128)(2,1)} %refs_1_.1), custom_call_target="tpu_custom_call" | custom-call | bytes 73400320 | tf_op jit(solution)/shard_map/pallas_call | solution.py:226
  58.9 8.5 %all-gather.4.cloned.1.call-done = bf16[1168,1024]{1,0:T(8,128)(2,1)} async-done(((bf16[1168,256]{1,0:T(8,128)(2,1)}), bf16[1168,1024]{1,0:T(8,128)(2,1)}) %all-gather.4.cloned.1.call-update) | async-done | bytes 2392080 | tf_op jit(solution)/shard_map/all_gather | solution.py:283
  74.0 10.8 %shard_map.255 = (bf16[1024,256]{1,0:T(8,128)(2,1)}, f32[2,2,1024]{2,1,0:T(2,128)S(1)}) custom-call(s32[1024]{0:T(1024)S(1)} %copy-done, f32[4]{0:T(128)S(1)} %multiply_power_fusion.slope_ref, bf16[1024,768]{1,0:T(8,128)(2,1)S(1)} %add_convert_fusion.2.packed_ref), custom_call_target="tpu_custom_call" | custom-call | flops 1073741824 | bytes 3145728 | tf_op jit(solution)/shard_map/pallas_call | solution.py:126
  88.3 48.5 %shard_map.256 = (bf16[8,128,1024]{2,1,0:T(8,128)(2,1)}, bf16[8,128,1024]{2,1,0:T(8,128)(2,1)}) custom-call(bf16[128,1024]{1,0:T(8,128)(2,1)} %slice.81.refs_0_, bf16[128,1024]{1,0:T(8,128)(2,1)} %bitcast.53), custom_call_target="tpu_custom_call" | custom-call | bytes 83886080 | tf_op jit(solution)/shard_map/pallas_call | solution.py:226
  136.8 5.5 %fusion.34 = (f32[1024]{0:T(1024)S(1)}, f32[1024,1024]{1,0:T(8,128)S(1)}) fusion(f32[1024]{0:T(1024)S(1)} %bitcast.69, bf16[1024,1024]{1,0:T(8,128)(2,1)} %all-gather.6.cloned.1.call-done, bf16[1024,1024]{1,0:T(8,128)(2,1)} %bitcast.56, bf16[1168,1024]{1,0:T(8,128)(2,1)} %all-gather.4.cloned.1.call-done), kind=kOutput, calls=%fused_computation.91 | convolution fusion | flops 2151676928 | bytes 10493952 | tf_op jit(solution)/shard_map/dot_general | solution.py:40
  145.4 4.4 fusion.27
  149.8 25.6 %all-gather.8.cloned.1.call-done = bf16[1024,1024]{1,0:T(8,128)(2,1)} async-done(((bf16[1024,256]{1,0:T(8,128)(2,1)}), bf16[1024,1024]{1,0:T(8,128)(2,1)}) %all-gather.8.cloned.1.call-update) | async-done | bytes 2097168 | tf_op jit(solution)/shard_map/all_gather | solution.py:292
  175.4 8.3 %convert_reduce_fusion.4 = (f32[1024]{0:T(1024)S(1)}, bf16[1024,1024]{1,0:T(8,128)(2,1)S(1)}) fusion(f32[1024,1024]{1,0:T(8,128)} %fusion.27, f32[1024]{0:T(1024)S(1)} %convert_element_type.120, bf16[1024,1024]{1,0:T(8,128)(2,1)} %all-gather.8.cloned.1.call-done, bf16[1024,1024]{1,0:T(8,128)(2,1)} %bitcast.72), kind=kOutput, calls=%fused_computation.33 | convolution fusion | flops 2171599872 | bytes 10493952 | tf_op jit(solution)/shard_map/dot_general | solution.py:314
  185.1 3.7 convolution_convert_fusion.2
  189.1 7.0 %convolution_convert_fusion.3 = bf16[1024,1024]{1,0:T(8,128)(2,1)} fusion(bf16[1024,1024]{1,0:T(8,128)(2,1)} %bitcast.73, f32[1024,1024]{1,0:T(8,128)} %fusion.27, f32[1024]{0:T(1024)S(1)} %convert_element_type.120), kind=kOutput, calls=%fused_computation.49 | convolution fusion | flops 2159017984 | bytes 8392704 | tf_op jit(solution)/shard_map/dot_general | solution.py:40
  196.4 6.9 %convolution_convert_fusion = bf16[1024,1024]{0,1:T(8,128)(2,1)} fusion(bf16[1024,1024]{1,0:T(8,128)(2,1)} %all-gather.8.cloned.1.call-done, f32[1024,1024]{1,0:T(8,128)} %fusion.27, f32[1024]{0:T(1024)S(1)} %convert_element_type.120), kind=kOutput, calls=%fused_computation.46 | convolution fusion | flops 2159017984 | bytes 8392704 | tf_op jit(solution)/shard_map/dot_general | solution.py:40
  203.3 70.4 %all-reduce.4.cloned.1.call-done = bf16[1024,1024]{1,0:T(8,128)(2,1)} async-done(((bf16[1024,1024]{1,0:T(8,128)(2,1)}), bf16[1024,1024]{1,0:T(8,128)(2,1)}) %all-reduce.4.cloned.1.call-update) | async-done | bytes 2097168 | tf_op jit(solution)/shard_map/psum | solution.py:317
  273.7 4.5 fusion.17
  278.5 3.1 convert_reduce_fusion.5
  283.8 12.8 %shard_map.257 = bf16[1024,768]{1,0:T(8,128)(2,1)S(1)} custom-call(s32[1024]{0:T(1024)S(1)} %copy-done, f32[4]{0:T(128)S(1)} %multiply_power_fusion.slope_ref, bf16[1024,768]{1,0:T(8,128)(2,1)S(1)} %add_convert_fusion.2.packed_ref, f32[2,2,1024]{2,1,0:T(2,128)S(1)} %get-tuple-element.29.total_ref, bf16[1024,256]{1,0:T(8,128)(2,1)S(1)} %convolution_convert_fusion.6.grad_ref), custom_call_target="tpu_custom_call" | custom-call | flops 2684354560 | bytes 4718592 | tf_op jit(solution)/shard_map/pallas_call | solution.py:148
  296.6 4.9 %multiply_reduce_fusion = (f32[1024]{0:T(1024)S(1)}, f32[1024]{0:T(1024)S(1)}, f32[1024]{0:T(1024)S(1)}, f32[1024]{0:T(1024)S(1)}, bf16[1024,1024]{1,0:T(8,128)(2,1)}, /*index=5*/f32[1024,1024]{1,0:T(8,128)}) fusion(f32[1024]{0:T(1024)S(1)} %add_rsqrt_fusion.1, f32[1024]{0:T(1024)S(1)} %broadcast_multiply_fusion.4, bf16[1168,1024]{1,0:T(8,128)(2,1)S(1)} %copy-done.6, ...), kind=kOutput, calls=%fused_computation.35 | convolution fusion | flops 1622142976 | bytes 11563008 | tf_op jit(solution)/shard_map/dot_general | solution.py:40
  301.5 6.9 %convolution_convert_fusion.1 = bf16[1024,1024]{1,0:T(8,128)(2,1)} fusion(bf16[1024,1024]{1,0:T(8,128)(2,1)} %copy-done.17, f32[1024,1024]{1,0:T(8,128)} %copy-done.2, f32[1024]{0:T(1024)S(1)} %bitcast.68, f32[1024]{0:T(1024)S(1)} %bitcast.61, f32[1024]{0:T(1024)S(1)} %add_rsqrt_fusion, f32[1024]{0:T(1024)S(1)} %broadcast_multiply_fusion.3), kind=kOutput, calls=%fused_computation.47 | convolution fusion | flops 2153775104 | bytes 8404992 | tf_op jit(solution)/shard_map/dot_general | solution.py:40
  308.5 48.5 %shard_map.259 = (bf16[8,128,1024]{2,1,0:T(8,128)(2,1)}, bf16[8,128,1024]{2,1,0:T(8,128)(2,1)}) custom-call(bf16[8,128,1024]{2,1,0:T(8,128)(2,1)} %bitcast.50, bf16[8,128,1024]{2,1,0:T(8,128)(2,1)} %bitcast.49), custom_call_target="tpu_custom_call" | custom-call | bytes 83886080 | tf_op jit(solution)/shard_map/pallas_call | solution.py:226
  363.2 16.7 %all-reduce.1 = (f32[1024]{0:T(1024)S(1)}, f32[1024]{0:T(1024)S(1)}, f32[1024]{0:T(1024)S(1)}, f32[1024]{0:T(1024)S(1)}) all-reduce(f32[1024]{0:T(1024)S(1)} %get-tuple-element.49, f32[1024]{0:T(1024)S(1)} %get-tuple-element.52, f32[1024]{0:T(1024)S(1)} %get-tuple-element.48, ...), channel_id=1, replica_groups=mesh['wide'=8,'narrow'=4] {'narrow'}, use_global_device_ids=true, to_apply=%region_12.13 | all-reduce | flops 4096 | bytes 32768 | tf_op jit(solution)/shard_map/psum | solution.py:356
  380.4 22.3 %psum.47 = f32[3072]{0:T(1024)S(1)} all-reduce(f32[3072]{0:T(1024)S(1)} %constant_dynamic-update-slice_fusion), channel_id=1, replica_groups=mesh['wide'=8,'narrow'=4] {'wide'}, use_global_device_ids=true, to_apply=%region_23.24 | all-reduce | flops 3072 | bytes 24576 | tf_op jit(solution)/shard_map/psum | solution.py:378
  403.9 3.9 convolution_convert_fusion.5
  407.7 3.5 convolution_convert_fusion.4
  411.3 24.3 %shard_map.258 = (bf16[8,128,768]{2,1,0:T(8,128)(2,1)}, bf16[8,128,256]{2,1,0:T(8,128)(2,1)}) custom-call(bf16[8,128,768]{2,1,0:T(8,128)(2,1)} %bitcast.52, bf16[8,128,256]{2,1,0:T(8,128)(2,1)} %bitcast.51), custom_call_target="tpu_custom_call" | custom-call | bytes 41943040 | tf_op jit(solution)/shard_map/pallas_call | solution.py:226
  442.7 3.0 add_convert_fusion.3
  (107 shorter events, 39.7 us)
Async XLA Ops:
  7.2 60.2 %all-gather.4.cloned.1.call-start = ((), (), s32[]{:S(2)}) async-start(), calls=%async_computation.2 | async-start | bytes 2990080 | tf_op jit(solution)/shard_map/all_gather | solution.py:283
  13.4 123.4 %all-gather.6.cloned.1.call-start = ((), (), s32[]{:S(2)}) async-start(), calls=%async_computation.3 | async-start | bytes 2621440 | tf_op jit(solution)/shard_map/all_gather | solution.py:304
  58.9 12.9 %copy-start.13 = (bf16[8,128,768]{2,1,0:T(8,128)(2,1)S(1)}, bf16[8,128,768]{2,1,0:T(8,128)(2,1)}, u32[]{:S(2)}) copy-start(bf16[8,128,768]{2,1,0:T(8,128)(2,1)} %get-tuple-element.24) | copy-start | bytes 4718596
  67.4 4.4 copy-start.5
  71.8 2.2 copy-start
  74.0 11.8 %copy-start.10 = (bf16[1024]{0:T(1024)(128)(2,1)S(1)}, bf16[1024]{0:T(1024)(128)(2,1)}, u32[]{:S(2)}) copy-start(bf16[1024]{0:T(1024)(128)(2,1)} %param.26) | copy-start | bytes 6148
  74.0 11.8 %copy-start.9 = (bf16[1024,128]{1,0:T(8,128)(2,1)S(1)}, bf16[1024,128]{1,0:T(8,128)(2,1)}, u32[]{:S(2)}) copy-start(bf16[1024,128]{1,0:T(8,128)(2,1)} %param.27) | copy-start | bytes 786436
  84.8 90.7 %all-gather.8.cloned.1.call-start = ((), (), s32[]{:S(2)}) async-start(), calls=%async_computation.5 | async-start | bytes 2621440 | tf_op jit(solution)/shard_map/all_gather | solution.py:292
  85.5 188.2 %all-reduce.4.cloned.1.call-start = ((), (), s32[]{:S(2)}) async-start(), calls=%async_computation.6 | async-start | bytes 4194304 | tf_op jit(solution)/shard_map/psum | solution.py:317
  142.3 2.1 copy-start.2
  142.3 3.1 copy-start.11
  175.4 9.7 %copy-start.12 = (bf16[8,128,1024]{2,1,0:T(8,128)(2,1)S(1)}, bf16[8,128,1024]{2,1,0:T(8,128)(2,1)}, u32[]{:S(2)}) copy-start(bf16[8,128,1024]{2,1,0:T(8,128)(2,1)} %get-tuple-element.27) | copy-start | bytes 6291460
  183.8 1.3 copy-start.17
  188.8 7.4 %copy-start.15 = (bf16[256]{0:T(256)(128)(2,1)S(1)}, bf16[256]{0:T(256)(128)(2,1)}, u32[]{:S(2)}) copy-start(bf16[256]{0:T(256)(128)(2,1)} %param.17) | copy-start | bytes 1540
  188.9 7.4 %copy-start.16 = (bf16[256]{0:T(256)(128)(2,1)S(1)}, bf16[256]{0:T(256)(128)(2,1)}, u32[]{:S(2)}) copy-start(bf16[256]{0:T(256)(128)(2,1)} %param.28) | copy-start | bytes 1540
  188.9 7.4 %copy-start.8 = (bf16[1024,256]{1,0:T(8,128)(2,1)S(1)}, bf16[1024,256]{1,0:T(8,128)(2,1)}, u32[]{:S(2)}) copy-start(bf16[1024,256]{1,0:T(8,128)(2,1)} %param.29) | copy-start | bytes 1572868
  188.9 251.5 %reduce-scatter.3.cloned.1.call-start = ((), (), s32[]{:S(2)}) async-start(), calls=%async_computation.4 | async-start | bytes 2621440 | tf_op jit(solution)/shard_map/reduce_scatter | solution.py:320
  196.2 246.5 %reduce-scatter.5.cloned.1.call-start = ((), (), s32[]{:S(2)}) async-start(), calls=%async_computation.7 | async-start | bytes 2621440 | tf_op jit(solution)/shard_map/reduce_scatter | solution.py:352
  273.7 4.5 copy-start.3
  273.7 4.7 %copy-start.4 = (bf16[1024,1024]{1,0:T(8,128)(2,1)S(1)}, bf16[1024,1024]{1,0:T(8,128)(2,1)}, u32[]{:S(2)}) copy-start(bf16[1024,1024]{1,0:T(8,128)(2,1)} %all-reduce.4.cloned.1.call-done) | copy-start | bytes 6291460
  281.6 2.2 copy-start.1
  283.8 12.9 %copy-start.6 = (bf16[1168,1024]{1,0:T(8,128)(2,1)S(1)}, bf16[1168,1024]{1,0:T(8,128)(2,1)}, u32[]{:S(2)}) copy-start(bf16[1168,1024]{1,0:T(8,128)(2,1)} %all-gather.4.cloned.1.call-done) | copy-start | bytes 7176196
  283.8 12.9 %copy-start.14 = (bf16[8,128,768]{2,1,0:T(8,128)(2,1)S(1)}, bf16[8,128,768]{2,1,0:T(8,128)(2,1)}, u32[]{:S(2)}) copy-start(bf16[8,128,768]{2,1,0:T(8,128)(2,1)} %get-tuple-element.24) | copy-start | bytes 4718596
  402.7 5.0 %copy-start.7 = (bf16[1168,1024]{1,0:T(8,128)(2,1)S(1)}, bf16[1168,1024]{1,0:T(8,128)(2,1)}, u32[]{:S(2)}) copy-start(bf16[1168,1024]{1,0:T(8,128)(2,1)} %all-gather.4.cloned.1.call-done) | copy-start | bytes 7176196
Sparse Core Ops, SparseCore 0:
  13.5 53.7 all-gather.3
  84.9 44.4 all-gather.5
  130.9 44.4 all-gather.7
  189.0 84.7 all-reduce.3
  276.0 42.7 reduce-scatter.2
  321.0 43.1 reduce-scatter.4

commit v2 on v1

--- a/solution.py
+++ b/solution.py
@@ -164,17 +164,18 @@
     )(segments, slopes, packed, log_totals, grad_attended)
 
 
-def exchange_body(scatter, count, devices, *refs):
+def exchange_body(scatter, axis, devices, *refs):
+    count = len(scatter)
     sources, results = refs[:count], refs[count : 2 * count]
     local_sem, send_sem, recv_sem = refs[2 * count :]
-    me = lax.axis_index("wide")
+    me = lax.axis_index(axis)
 
     barrier = pltpu.get_barrier_semaphore()
 
     def greet(step, carry):
         peer = lax.rem(me + step, devices)
         pl.semaphore_signal(
-            barrier, inc=1, device_id={"wide": peer}, device_id_type=pl.DeviceIdType.MESH
+            barrier, inc=1, device_id={axis: peer}, device_id_type=pl.DeviceIdType.MESH
         )
         return carry
 
@@ -182,7 +183,7 @@
     pl.semaphore_wait(barrier, devices - 1)
 
     def block_of(item, owner):
-        return sources[item].at[owner] if scatter else sources[item]
+        return sources[item].at[owner] if scatter[item] else sources[item]
 
     def copy_to(item, step):
         peer = lax.rem(me + step, devices)
@@ -191,7 +192,7 @@
             dst_ref=results[item].at[me],
             send_sem=send_sem.at[item, step],
             recv_sem=recv_sem.at[item, step],
-            device_id={"wide": peer},
+            device_id={axis: peer},
             device_id_type=pl.DeviceIdType.MESH,
         )
 
@@ -218,13 +219,13 @@
     lax.fori_loop(1, devices, finish, 0)
 
 
-def exchange(sources, scatter, call_id):
-    devices = lax.axis_size("wide")
+def exchange(sources, scatter, axis, call_id):
+    devices = lax.axis_size(axis)
     count = len(sources)
-    shapes = [item.shape[1:] if scatter else item.shape for item in sources]
+    shapes = [item.shape[1:] if apart else item.shape for apart, item in zip(scatter, sources)]
     size = sum(devices * rows * width * 2 for rows, width in shapes)
     return pl.pallas_call(
-        partial(exchange_body, scatter, count, devices),
+        partial(exchange_body, scatter, axis, devices),
         in_specs=[pl.BlockSpec(memory_space=pl.ANY)] * count,
         out_specs=[pl.BlockSpec(memory_space=pl.ANY)] * count,
         out_shape=[
@@ -242,17 +243,16 @@
 
 
 def gather_rows(sources, call_id):
-    return [
-        item.reshape(-1, item.shape[-1]) for item in exchange(sources, False, call_id)
-    ]
-
-
-def scatter_sums(sources, call_id):
+    gathered = exchange(sources, (False,) * len(sources), "wide", call_id)
+    return [item.reshape(-1, item.shape[-1]) for item in gathered]
+
+
+def scatter_sums(sources, call_id, whole=()):
     devices = lax.axis_size("wide")
     blocks = [item.reshape(devices, -1, item.shape[-1]) for item in sources]
-    return [
-        jnp.sum(item.astype(jnp.float32), axis=0) for item in exchange(blocks, True, call_id)
-    ]
+    scatter = (True,) * len(blocks) + (False,) * len(whole)
+    parts = exchange([*blocks, *whole], scatter, "wide", call_id)
+    return [jnp.sum(item.astype(jnp.float32), axis=0) for item in parts]
 
 
 def local(
@@ -316,7 +316,7 @@
     grad_pre = gelu_back(grad_hidden)[0].astype(jnp.bfloat16)
     grad_act_two = lax.psum(
         contract(grad_pre, up_full, 1, 1).astype(jnp.bfloat16), "narrow"
-    ).astype(jnp.float32)
+    )
     mlp_out = lax.psum_scatter(
         contract(hidden, down_rows, 1, 1).astype(jnp.bfloat16),
         "narrow",
@@ -331,6 +331,10 @@
     grad_down = contract(grad_out, hidden, 0, 0).astype(jnp.bfloat16)
     grad_up = contract(act_two, grad_pre, 0, 0).astype(jnp.bfloat16)
     up_weight_grad, down_rows_grad = scatter_sums([grad_up, grad_down], 2)
+    grad_act_two, up_weight_grad, down_rows_grad = lax.optimization_barrier(
+        (grad_act_two, up_weight_grad, down_rows_grad)
+    )
+    grad_act_two = grad_act_two.astype(jnp.float32)
     second_gain_grad = own_columns(jnp.sum(grad_act_two * hat_two, axis=0), col_start, local_width)
     second_shift_grad = own_columns(jnp.sum(grad_act_two, axis=0), col_start, local_width)
     grad_residual = grad_out.astype(jnp.float32) + norm_backward(
@@ -353,18 +357,17 @@
         grad_one_part.astype(jnp.bfloat16), "narrow", scatter_dimension=1, tiled=True
     ).astype(jnp.float32)
     scaled_part = grad_one_part * gain_one
-    sum_plain, sum_hat, gain_part, shift_part = lax.psum(
-        (
-            jnp.sum(scaled_part, axis=1),
-            jnp.sum(scaled_part * hat_one, axis=1),
-            jnp.sum(grad_one_part * hat_one, axis=0),
-            jnp.sum(grad_one_part, axis=0),
-        ),
-        "narrow",
-    )
+    row_sums = jnp.stack([jnp.sum(scaled_part, axis=1), jnp.sum(scaled_part * hat_one, axis=1)])
+    feature_sums = jnp.stack(
+        [jnp.sum(grad_one_part * hat_one, axis=0), jnp.sum(grad_one_part, axis=0)]
+    )
+    lines = jnp.concatenate([row_sums.reshape(-1, 128), feature_sums.reshape(-1, 128)], axis=0)
+    (line_parts,) = exchange([lines], (False,), "narrow", 4)
+    flat_sums = jnp.sum(line_parts, axis=0).reshape(-1)
+    sum_plain, sum_hat = flat_sums[: 2 * tok_rows].reshape(2, tok_rows)
+    gain_part, shift_part = flat_sums[2 * tok_rows :].reshape(2, -1)
     grad_qkv = contract(act_one, grad_packed, 0, 0).astype(jnp.bfloat16)
     grad_dense = contract(grad_branch, attended, 0, 0).astype(jnp.bfloat16)
-    qkv_weight_grad, dense_rows_grad = scatter_sums([grad_qkv, grad_dense], 3)
     small = (
         own_columns(gain_part, col_start, local_width),
         own_columns(shift_part, col_start, local_width),
@@ -375,7 +378,10 @@
         up_bias_grad,
         down_bias_grad,
     )
-    small_sums = lax.psum(jnp.concatenate(small), "wide")
+    qkv_weight_grad, dense_rows_grad, small_sums = scatter_sums(
+        [grad_qkv, grad_dense], 3, [jnp.concatenate(small).reshape(-1, 128)]
+    )
+    small_sums = small_sums.reshape(-1)
     bounds = [0]
     for item in small:
         bounds.append(bounds[-1] + item.shape[0])

time: 460 us -> 382 us (0.83)
  waiting for transfers between devices: 105 us -> 57.9 us
  blocking collectives: 39 us -> 0 us
  Pallas kernels: 189 us -> 199 us
    psum x1, waiting for transfers between devices: 70.4 us -> 13.5 us  [local(): lax.psum(contract(grad_pre, up_full, 1, 1).astype(jnp.bfloat16), 'narrow')]
    psum x2 -> x0, blocking collectives: 39 us -> none  [the longest x1 22.3 us: local(): small_sums = lax.psum(jnp.concatenate(small), 'wide')]
    pallas_call x4 -> x5, Pallas kernels: 166 us -> 176 us  [exchange(): pl.pallas_call(partial(exchange_body, scatter, axis, devices), in_specs=[...]
    reduce_scatter x1, waiting for transfers between devices: 0.01 us -> 9.49 us  [local(): lax.psum_scatter(grad_one_part.astype(jnp.bfloat16), 'narrow', scatter_di...]
    reduce_sum x4 -> x5, other arithmetic: 8.31 us -> 9.44 us  [the longest x4 8.59 us: scatter_sums(): return [jnp.sum(item.astype(jnp.float32), axis=0) for item in parts]]
  transfers between devices with their start and end apart: 6 -> 6, of which waited for: 3 -> 4; matrix products, arithmetic and copies ran while one was open for 16% -> 19% of each run, Pallas kernels for 39% -> 50%
where the time goes in v2:
time: 382 us; the launch traced here: 376 us
  Pallas kernels  199 us (52%)
  waiting for transfers between devices  57.9 us (15%)
  matrix products  56.6 us (15%)
  other arithmetic  30.5 us (8%)
  local copies, waits for them, and re-layouts  15.8 us (4%)
  between operations  15.1 us (4%)
    pallas_call x5, Pallas kernels, exchange(): pl.pallas_call(partial(exchange_body, scatter, axis, devices), in_specs=[...  176 us
    dot_general x8, matrix products, contract(): lax.dot_general(left, right, (((left_dim,), (right_dim,)), ((), ())), pre...  39.5 us
    all_gather x1, waiting for transfers between devices, local(): grad_out = lax.all_gather(cotangent, 'narrow', axis=1, tiled=True)  25.6 us
    psum x1, waiting for transfers between devices, local(): lax.psum(contract(grad_pre, up_full, 1, 1).astype(jnp.bfloat16), 'narrow')  13.5 us
    pallas_call x1, Pallas kernels, attend_backward(): pl.pallas_call(backward_body, grid=(heads_here // head_group,), in_specs=...  12.8 us
    pallas_call x1, Pallas kernels, attend_forward(): pl.pallas_call(forward_body, grid=(groups,), in_specs=[scalars, scalars,...  10.8 us
    reduce_scatter x1, waiting for transfers between devices, local(): lax.psum_scatter(grad_one_part.astype(jnp.bfloat16), 'narrow', scatter_di...  9.49 us
    reduce_sum x4, other arithmetic, scatter_sums(): return [jnp.sum(item.astype(jnp.float32), axis=0) for item in parts]  8.59 us
  transfers between devices with their start and end apart: 6, of which 4 were waited for; matrix products, arithmetic and copies ran while one was open for 19% of the time, Pallas kernels for 50%

profile of v2, /device:TPU:0, one launch (start us, length us, event | category | flops | bytes accessed | tf_op | source)
XLA Modules:
  0.0 375.6 jit_solution(14222081287028544617)
XLA Ops:
  14.5 44.4 %shard_map.254 = (bf16[8,128,768]{2,1,0:T(8,128)(2,1)}, bf16[8,128,1024]{2,1,0:T(8,128)(2,1)}) custom-call(bf16[128,768]{1,0:T(8,128)(2,1)} %refs_0_.1, bf16[128,1024]{1,0:T(8,128)(2,1)} %refs_1_.1), custom_call_target="tpu_custom_call" | custom-call | bytes 73400320 | tf_op jit(solution)/shard_map/pallas_call | solution.py:227
  58.9 8.5 %all-gather.4.cloned.1.call-done = bf16[1168,1024]{1,0:T(8,128)(2,1)} async-done(((bf16[1168,256]{1,0:T(8,128)(2,1)}), bf16[1168,1024]{1,0:T(8,128)(2,1)}) %all-gather.4.cloned.1.call-update) | async-done | bytes 2392080 | tf_op jit(solution)/shard_map/all_gather | solution.py:283
  74.0 10.8 %shard_map.255 = (bf16[1024,256]{1,0:T(8,128)(2,1)}, f32[2,2,1024]{2,1,0:T(2,128)S(1)}) custom-call(s32[1024]{0:T(1024)S(1)} %copy-done, f32[4]{0:T(128)S(1)} %multiply_power_fusion.slope_ref, bf16[1024,768]{1,0:T(8,128)(2,1)S(1)} %add_convert_fusion.2.packed_ref), custom_call_target="tpu_custom_call" | custom-call | flops 1073741824 | bytes 3145728 | tf_op jit(solution)/shard_map/pallas_call | solution.py:126
  88.3 48.5 %shard_map.256 = (bf16[8,128,1024]{2,1,0:T(8,128)(2,1)}, bf16[8,128,1024]{2,1,0:T(8,128)(2,1)}) custom-call(bf16[128,1024]{1,0:T(8,128)(2,1)} %slice.125.refs_0_, bf16[128,1024]{1,0:T(8,128)(2,1)} %bitcast.82), custom_call_target="tpu_custom_call" | custom-call | bytes 83886080 | tf_op jit(solution)/shard_map/pallas_call | solution.py:227
  136.8 5.5 %fusion.34 = (f32[1024]{0:T(1024)S(1)}, f32[1024,1024]{1,0:T(8,128)S(1)}) fusion(f32[1024]{0:T(1024)S(1)} %bitcast.99, bf16[1024,1024]{1,0:T(8,128)(2,1)} %all-gather.6.cloned.1.call-done, bf16[1024,1024]{1,0:T(8,128)(2,1)} %bitcast.85, bf16[1168,1024]{1,0:T(8,128)(2,1)} %all-gather.4.cloned.1.call-done), kind=kOutput, calls=%fused_computation.105 | convolution fusion | flops 2151676928 | bytes 10493952 | tf_op jit(solution)/shard_map/dot_general | solution.py:40
  145.4 4.4 %fusion.28 = f32[1024,1024]{1,0:T(8,128)} fusion(bf16[1024,1024]{1,0:T(8,128)(2,1)S(1)} %bitcast.104, f32[1024,1024]{1,0:T(8,128)S(1)} %get-tuple-element.88, f32[1024]{0:T(1024)S(1)} %bitcast.97, f32[1024]{0:T(1024)S(1)} %bitcast.87, f32[1024]{0:T(1024)S(1)} %add_rsqrt_fusion, f32[1024]{0:T(1024)S(1)} %broadcast_multiply_fusion.2), kind=kOutput, calls=%fused_computation.102 | convolution fusion | flops 2152726528 | bytes 10502144 | tf_op jit(solution)/shard_map/dot_general | solution.py:310
  149.8 25.6 %all-gather.8.cloned.1.call-done = bf16[1024,1024]{1,0:T(8,128)(2,1)} async-done(((bf16[1024,256]{1,0:T(8,128)(2,1)}), bf16[1024,1024]{1,0:T(8,128)(2,1)}) %all-gather.8.cloned.1.call-update) | async-done | bytes 2097168 | tf_op jit(solution)/shard_map/all_gather | solution.py:292
  175.5 8.3 %convert_reduce_fusion.2 = (f32[1024]{0:T(1024)S(1)}, bf16[1024,1024]{1,0:T(8,128)(2,1)S(1)}) fusion(f32[1024,1024]{1,0:T(8,128)} %fusion.28, f32[1024]{0:T(1024)S(1)} %convert_element_type.120, bf16[1024,1024]{1,0:T(8,128)(2,1)} %all-gather.8.cloned.1.call-done, bf16[1024,1024]{1,0:T(8,128)(2,1)} %bitcast.106), kind=kOutput, calls=%fused_computation.31 | convolution fusion | flops 2171599872 | bytes 10493952 | tf_op jit(solution)/shard_map/dot_general | solution.py:314
  185.1 3.7 convolution_convert_fusion.2
  189.1 7.0 %convolution_convert_fusion.3 = bf16[1024,1024]{1,0:T(8,128)(2,1)} fusion(bf16[1024,1024]{1,0:T(8,128)(2,1)} %bitcast.107, f32[1024,1024]{1,0:T(8,128)} %fusion.28, f32[1024]{0:T(1024)S(1)} %convert_element_type.120), kind=kOutput, calls=%fused_computation.49 | convolution fusion | flops 2159017984 | bytes 8392704 | tf_op jit(solution)/shard_map/dot_general | solution.py:40
  196.2 7.1 %convolution_convert_fusion.1 = bf16[1024,1024]{1,0:T(8,128)(2,1)} fusion(bf16[1024,1024]{1,0:T(8,128)(2,1)} %copy-done.21, f32[1024,1024]{1,0:T(8,128)} %copy-done.2, f32[1024]{0:T(1024)S(1)} %bitcast.98, f32[1024]{0:T(1024)S(1)} %bitcast.88, f32[1024]{0:T(1024)S(1)} %add_rsqrt_fusion, f32[1024]{0:T(1024)S(1)} %broadcast_multiply_fusion.2), kind=kOutput, calls=%fused_computation.47 | convolution fusion | flops 2153775104 | bytes 8404992 | tf_op jit(solution)/shard_map/dot_general | solution.py:40
  203.3 4.0 %convolution_convert_fusion = bf16[1024,1024]{0,1:T(8,128)(2,1)} fusion(bf16[1024,1024]{1,0:T(8,128)(2,1)S(1)} %copy-done.10, f32[1024,1024]{1,0:T(8,128)S(1)} %copy-done.20, f32[1024]{0:T(1024)S(1)} %convert_element_type.120), kind=kOutput, calls=%fused_computation.46 | convolution fusion | flops 2159017984 | bytes 8392704 | tf_op jit(solution)/shard_map/dot_general | solution.py:40
  207.3 48.8 %shard_map.257 = (bf16[8,128,1024]{2,1,0:T(8,128)(2,1)}, bf16[8,128,1024]{2,1,0:T(8,128)(2,1)}) custom-call(bf16[8,128,1024]{2,1,0:T(8,128)(2,1)} %bitcast.78, bf16[8,128,1024]{2,1,0:T(8,128)(2,1)} %bitcast.79), custom_call_target="tpu_custom_call" | custom-call | bytes 83886080 | tf_op jit(solution)/shard_map/pallas_call | solution.py:227
  256.1 4.2 %convert_reduce_fusion.4 = (f32[128,1024]{1,0:T(8,128)}, f32[128,1024]{1,0:T(8,128)}) fusion(bf16[8,128,1024]{2,1,0:T(8,128)(2,1)} %get-tuple-element.34, bf16[8,128,1024]{2,1,0:T(8,128)(2,1)} %get-tuple-element.33), kind=kLoop, calls=%fused_computation.35 | loop fusion | flops 3932160 | bytes 5242880 | tf_op jit(solution)/shard_map/reduce_sum | solution.py:255
  260.2 13.5 %all-reduce.3.cloned.1.call-done = bf16[1024,1024]{1,0:T(8,128)(2,1)} async-done(((bf16[1024,1024]{1,0:T(8,128)(2,1)}), bf16[1024,1024]{1,0:T(8,128)(2,1)}) %all-reduce.3.cloned.1.call-update) | async-done | bytes 2097168 | tf_op jit(solution)/shard_map/psum | solution.py:317
  273.8 4.6 %fusion.17 = (f32[1024]{0:T(1024)S(1)}, f32[1024]{0:T(1024)S(1)}, f32[1024]{0:T(1024)S(1)}, f32[1024]{0:T(1024)S(1)}) fusion(bf16[1024,1024]{1,0:T(8,128)(2,1)} %all-reduce.3.cloned.1.call-done, f32[1024,1024]{1,0:T(8,128)} %copy-done.2, f32[1024]{0:T(1024)S(1)} %add_rsqrt_fusion, f32[1024]{0:T(1024)S(1)} %broadcast_multiply_fusion.2, f32[1024]{0:T(1024)S(1)} %bitcast.89), kind=kLoop, calls=%fused_computation.25 | loop fusion | flops 10481664 | bytes 6320128 | tf_op jit(solution)/shard_map/reduce_sum | solution.py:338
  278.5 3.1 convert_reduce_fusion.3
  283.8 12.8 %shard_map.258 = bf16[1024,768]{1,0:T(8,128)(2,1)S(1)} custom-call(s32[1024]{0:T(1024)S(1)} %copy-done, f32[4]{0:T(128)S(1)} %multiply_power_fusion.slope_ref, bf16[1024,768]{1,0:T(8,128)(2,1)S(1)} %add_convert_fusion.2.packed_ref, f32[2,2,1024]{2,1,0:T(2,128)S(1)} %get-tuple-element.36.total_ref, bf16[1024,256]{1,0:T(8,128)(2,1)S(1)} %convolution_convert_fusion.6.grad_ref), custom_call_target="tpu_custom_call" | custom-call | flops 2684354560 | bytes 4718592 | tf_op jit(solution)/shard_map/pallas_call | solution.py:148
  296.7 4.6 %multiply_reduce_fusion.1 = (f32[1024]{0:T(1024)S(1)}, f32[1024]{0:T(1024)S(1)}, f32[1024]{0:T(1024)S(1)}, f32[1024]{0:T(1024)S(1)}, bf16[1024,1024]{1,0:T(8,128)(2,1)}, /*index=5*/f32[1024,1024]{1,0:T(8,128)}) fusion(f32[1024]{0:T(1024)S(1)} %bitcast.95, f32[1024]{0:T(1024)S(1)} %add_rsqrt_fusion.1, f32[1024]{0:T(1024)S(1)} %broadcast_multiply_fusion.3, ...), kind=kOutput, calls=%fused_computation.34 | convolution fusion | flops 1622142976 | bytes 11563008 | tf_op jit(solution)/shard_map/dot_general | solution.py:40
  302.3 6.7 %shard_map.259 = f32[4,32,128]{2,1,0:T(8,128)} custom-call(f32[32,128]{1,0:T(8,128)} %pad_maximum_fusion.refs_0_), custom_call_target="tpu_custom_call" | custom-call | bytes 655360 | tf_op jit(solution)/shard_map/pallas_call | solution.py:227
  310.8 4.1 %convolution_convert_fusion.5 = bf16[1024,256]{1,0:T(8,128)(2,1)} fusion(bf16[1024,256]{1,0:T(8,128)(2,1)} %get-tuple-element.29, f32[1024,1024]{1,0:T(8,128)} %copy-done.1), kind=kOutput, calls=%fused_computation.51 | convolution fusion | flops 538181632 | bytes 5242880 | tf_op jit(solution)/shard_map/dot_general | solution.py:40
  314.9 3.5 convolution_convert_fusion.4
  318.4 27.1 %shard_map.260 = (bf16[8,128,768]{2,1,0:T(8,128)(2,1)}, bf16[8,128,256]{2,1,0:T(8,128)(2,1)}, f32[8,24,128]{2,1,0:T(8,128)}) custom-call(bf16[8,128,768]{2,1,0:T(8,128)(2,1)} %bitcast.81, bf16[8,128,256]{2,1,0:T(8,128)(2,1)} %bitcast.80, f32[24,128]{1,0:T(8,128)} %bitcast.91), custom_call_target="tpu_custom_call" | custom-call | bytes 42926080 | tf_op jit(solution)/shard_map/pallas_call | solution.py:227
  355.8 9.5 %reduce-scatter.5.cloned.1.call-done = bf16[1024,256]{1,0:T(8,128)(2,1)} async-done(((bf16[1024,1024]{1,0:T(8,128)(2,1)}), bf16[1024,256]{1,0:T(8,128)(2,1)}) %reduce-scatter.5.cloned.1.call-update) | async-done | bytes 524304 | tf_op jit(solution)/shard_map/reduce_scatter | solution.py:356
  (121 shorter events, 40.2 us)
Async XLA Ops:
  7.2 60.2 %all-gather.4.cloned.1.call-start = ((), (), s32[]{:S(2)}) async-start(), calls=%async_computation.2 | async-start | bytes 2990080 | tf_op jit(solution)/shard_map/all_gather | solution.py:283
  13.4 123.4 %all-gather.6.cloned.1.call-start = ((), (), s32[]{:S(2)}) async-start(), calls=%async_computation.3 | async-start | bytes 2621440 | tf_op jit(solution)/shard_map/all_gather | solution.py:304
  67.4 4.4 %copy-start.5 = (bf16[1168,1024]{1,0:T(8,128)(2,1)S(1)}, bf16[1168,1024]{1,0:T(8,128)(2,1)}, u32[]{:S(2)}) copy-start(bf16[1168,1024]{1,0:T(8,128)(2,1)} %all-gather.4.cloned.1.call-done) | copy-start | bytes 7176196
  67.4 4.4 %copy-start.16 = (bf16[8,128,768]{2,1,0:T(8,128)(2,1)S(1)}, bf16[8,128,768]{2,1,0:T(8,128)(2,1)}, u32[]{:S(2)}) copy-start(bf16[8,128,768]{2,1,0:T(8,128)(2,1)} %get-tuple-element.28) | copy-start | bytes 4718596
  74.0 11.8 %copy-start.11 = (bf16[1024,128]{1,0:T(8,128)(2,1)S(1)}, bf16[1024,128]{1,0:T(8,128)(2,1)}, u32[]{:S(2)}) copy-start(bf16[1024,128]{1,0:T(8,128)(2,1)} %param.27) | copy-start | bytes 786436
  74.0 12.6 %copy-start.13 = (bf16[1024]{0:T(1024)(128)(2,1)S(1)}, bf16[1024]{0:T(1024)(128)(2,1)}, u32[]{:S(2)}) copy-start(bf16[1024]{0:T(1024)(128)(2,1)} %param.26) | copy-start | bytes 6148
  84.8 90.7 %all-gather.8.cloned.1.call-start = ((), (), s32[]{:S(2)}) async-start(), calls=%async_computation.5 | async-start | bytes 2621440 | tf_op jit(solution)/shard_map/all_gather | solution.py:292
  85.5 188.2 %all-reduce.3.cloned.1.call-start = ((), (), s32[]{:S(2)}) async-start(), calls=%async_computation.6 | async-start | bytes 4194304 | tf_op jit(solution)/shard_map/psum | solution.py:317
  142.3 3.1 copy-start.14
  175.5 9.7 %copy-start.15 = (bf16[8,128,1024]{2,1,0:T(8,128)(2,1)S(1)}, bf16[8,128,1024]{2,1,0:T(8,128)(2,1)}, u32[]{:S(2)}) copy-start(bf16[8,128,1024]{2,1,0:T(8,128)(2,1)} %get-tuple-element.31) | copy-start | bytes 6291460
  188.9 164.6 %reduce-scatter.3.cloned.1.call-start = ((), (), s32[]{:S(2)}) async-start(), calls=%async_computation.4 | async-start | bytes 2621440 | tf_op jit(solution)/shard_map/reduce_scatter | solution.py:320
  196.1 169.1 %reduce-scatter.5.cloned.1.call-start = ((), (), s32[]{:S(2)}) async-start(), calls=%async_computation.7 | async-start | bytes 2621440 | tf_op jit(solution)/shard_map/reduce_scatter | solution.py:356
  196.2 7.1 %copy-start.10 = (bf16[1024,1024]{1,0:T(8,128)(2,1)S(1)}, bf16[1024,1024]{1,0:T(8,128)(2,1)}, u32[]{:S(2)}) copy-start(bf16[1024,1024]{1,0:T(8,128)(2,1)} %all-gather.8.cloned.1.call-done) | copy-start | bytes 6291460
  196.2 7.1 %copy-start.20 = (f32[1024,1024]{1,0:T(8,128)S(1)}, f32[1024,1024]{1,0:T(8,128)}, u32[]{:S(2)}) copy-start(f32[1024,1024]{1,0:T(8,128)} %fusion.28) | copy-start | bytes 12582916
  273.8 4.6 %copy-start.3 = (f32[1024,1024]{1,0:T(8,128)S(1)}, f32[1024,1024]{1,0:T(8,128)}, u32[]{:S(2)}) copy-start(f32[1024,1024]{1,0:T(8,128)} %copy-done.2) | copy-start | bytes 12582916
  273.8 4.7 %copy-start.4 = (bf16[1024,1024]{1,0:T(8,128)(2,1)S(1)}, bf16[1024,1024]{1,0:T(8,128)(2,1)}, u32[]{:S(2)}) copy-start(bf16[1024,1024]{1,0:T(8,128)(2,1)} %all-reduce.3.cloned.1.call-done) | copy-start | bytes 6291460
  283.8 12.9 %copy-start.6 = (bf16[1168,1024]{1,0:T(8,128)(2,1)S(1)}, bf16[1168,1024]{1,0:T(8,128)(2,1)}, u32[]{:S(2)}) copy-start(bf16[1168,1024]{1,0:T(8,128)(2,1)} %all-gather.4.cloned.1.call-done) | copy-start | bytes 7176196
  283.8 12.9 %copy-start.17 = (bf16[8,128,768]{2,1,0:T(8,128)(2,1)S(1)}, bf16[8,128,768]{2,1,0:T(8,128)(2,1)}, u32[]{:S(2)}) copy-start(bf16[8,128,768]{2,1,0:T(8,128)(2,1)} %get-tuple-element.28) | copy-start | bytes 4718596
  296.7 4.7 %copy-start.9 = (bf16[1024,256]{1,0:T(8,128)(2,1)S(1)}, bf16[1024,256]{1,0:T(8,128)(2,1)}, u32[]{:S(2)}) copy-start(bf16[1024,256]{1,0:T(8,128)(2,1)} %param.29) | copy-start | bytes 1572868
  296.7 4.9 %copy-start.18 = (bf16[256]{0:T(256)(128)(2,1)S(1)}, bf16[256]{0:T(256)(128)(2,1)}, u32[]{:S(2)}) copy-start(bf16[256]{0:T(256)(128)(2,1)} %param.17) | copy-start | bytes 1540
  296.7 4.9 %copy-start.19 = (bf16[256]{0:T(256)(128)(2,1)S(1)}, bf16[256]{0:T(256)(128)(2,1)}, u32[]{:S(2)}) copy-start(bf16[256]{0:T(256)(128)(2,1)} %param.28) | copy-start | bytes 1540
  310.3 4.6 %copy-start.7 = (bf16[1168,1024]{1,0:T(8,128)(2,1)S(1)}, bf16[1168,1024]{1,0:T(8,128)(2,1)}, u32[]{:S(2)}) copy-start(bf16[1168,1024]{1,0:T(8,128)(2,1)} %all-gather.4.cloned.1.call-done) | copy-start | bytes 7176196
  310.8 7.7 %copy-start.12 = (f32[3072]{0:T(1024)}, f32[3072]{0:T(1024)S(1)}, u32[]{:S(2)}) copy-start(f32[3072]{0:T(1024)S(1)} %constant_dynamic-update-slice_fusion) | copy-start | bytes 36868
  314.9 33.4 %copy-start.8 = (f32[128,1024]{1,0:T(8,128)S(1)}, f32[128,1024]{1,0:T(8,128)}, u32[]{:S(2)}) copy-start(f32[128,1024]{1,0:T(8,128)} %get-tuple-element.41) | copy-start | bytes 1572868
  (4 other events, 7.9 us)
Sparse Core Ops, SparseCore 0:
  13.6 53.7 all-gather.3
  84.9 44.4 all-gather.5
  131.0 44.4 all-gather.7
  189.0 84.7 all-reduce.2
  276.0 43.8 reduce-scatter.2
  322.1 43.1 reduce-scatter.4

commit v3 on v2

--- a/solution.py
+++ b/solution.py
@@ -302,6 +302,7 @@
     ).astype(jnp.bfloat16)
     attended, log_totals = attend_forward(packed, slopes, segments)
     attended_full = lax.all_gather(attended, "narrow", axis=1, tiled=True)
+    dense_block, grad_out = lax.optimization_barrier((dense_block, grad_out))
     dense_rows, down_rows = gather_rows([dense_block, down_weight.T], 1)
     mixed = contract(attended_full, dense_rows, 1, 1)
     residual = inputs + (mixed + bias_dense)

time: 382 us -> 376 us (0.984)
  matrix products: 56.6 us -> 51.1 us
    unnamed x55 -> x59, local copies, waits for them, and re-layouts: 7.97 us -> 7.97 us
  transfers between devices with their start and end apart: 6 -> 6, of which waited for: 4 -> 4; matrix products, arithmetic and copies ran while one was open for 19% -> 18% of each run, Pallas kernels for 50% -> 54%
where the time goes in v3:
time: 376 us; the launch traced here: 370 us
  Pallas kernels  199 us (53%)
  waiting for transfers between devices  57.8 us (15%)
  matrix products  51.1 us (14%)
  other arithmetic  30.5 us (8%)
  local copies, waits for them, and re-layouts  15.8 us (4%)
  between operations  15.1 us (4%)
    pallas_call x5, Pallas kernels, exchange(): pl.pallas_call(partial(exchange_body, scatter, axis, devices), in_specs=[...  176 us
    dot_general x8, matrix products, contract(): lax.dot_general(left, right, (((left_dim,), (right_dim,)), ((), ())), pre...  39.3 us
    all_gather x1, waiting for transfers between devices, local(): grad_out = lax.all_gather(cotangent, 'narrow', axis=1, tiled=True)  25.8 us
    psum x1, waiting for transfers between devices, local(): lax.psum(contract(grad_pre, up_full, 1, 1).astype(jnp.bfloat16), 'narrow')  13.9 us
    pallas_call x1, Pallas kernels, attend_backward(): pl.pallas_call(backward_body, grid=(heads_here // head_group,), in_specs=...  12.8 us
    pallas_call x1, Pallas kernels, attend_forward(): pl.pallas_call(forward_body, grid=(groups,), in_specs=[scalars, scalars,...  10.8 us
    reduce_scatter x1, waiting for transfers between devices, local(): lax.psum_scatter(grad_one_part.astype(jnp.bfloat16), 'narrow', scatter_di...  9.51 us
    reduce_sum x4, other arithmetic, scatter_sums(): return [jnp.sum(item.astype(jnp.float32), axis=0) for item in parts]  8.59 us
  transfers between devices with their start and end apart: 6, of which 4 were waited for; matrix products, arithmetic and copies ran while one was open for 18% of the time, Pallas kernels for 54%

profile of v3, /device:TPU:0, one launch (start us, length us, event | category | flops | bytes accessed | tf_op | source)
XLA Modules:
  0.0 370.2 jit_solution(18268952386198838464)
XLA Ops:
  15.2 44.4 %shard_map.254 = (bf16[8,128,768]{2,1,0:T(8,128)(2,1)}, bf16[8,128,1024]{2,1,0:T(8,128)(2,1)}) custom-call(bf16[128,768]{1,0:T(8,128)(2,1)} %refs_0_.1, bf16[128,1024]{1,0:T(8,128)(2,1)} %refs_1_.1), custom_call_target="tpu_custom_call" | custom-call | bytes 73400320 | tf_op jit(solution)/shard_map/pallas_call | solution.py:227
  59.7 7.7 %all-gather.4.cloned.1.call-done = bf16[1168,1024]{1,0:T(8,128)(2,1)} async-done(((bf16[1168,256]{1,0:T(8,128)(2,1)}), bf16[1168,1024]{1,0:T(8,128)(2,1)}) %all-gather.4.cloned.1.call-update) | async-done | bytes 2392080 | tf_op jit(solution)/shard_map/all_gather | solution.py:283
  74.0 10.8 %shard_map.255 = (bf16[1024,256]{1,0:T(8,128)(2,1)}, f32[2,2,1024]{2,1,0:T(2,128)S(1)}) custom-call(s32[1024]{0:T(1024)S(1)} %copy-done, f32[4]{0:T(128)S(1)} %multiply_power_fusion.slope_ref, bf16[1024,768]{1,0:T(8,128)(2,1)S(1)} %add_convert_fusion.2.packed_ref), custom_call_target="tpu_custom_call" | custom-call | flops 1073741824 | bytes 3145728 | tf_op jit(solution)/shard_map/pallas_call | solution.py:126
  87.6 25.8 %all-gather.8.cloned.1.call-done = bf16[1024,1024]{1,0:T(8,128)(2,1)} async-done(((bf16[1024,256]{1,0:T(8,128)(2,1)}), bf16[1024,1024]{1,0:T(8,128)(2,1)}) %all-gather.8.cloned.1.call-update) | async-done | bytes 2097168 | tf_op jit(solution)/shard_map/all_gather | solution.py:292
  113.4 48.5 %shard_map.256 = (bf16[8,128,1024]{2,1,0:T(8,128)(2,1)}, bf16[8,128,1024]{2,1,0:T(8,128)(2,1)}) custom-call(bf16[128,1024]{1,0:T(8,128)(2,1)} %slice.125.refs_0_, bf16[128,1024]{1,0:T(8,128)(2,1)} %bitcast.67), custom_call_target="tpu_custom_call" | custom-call | bytes 83886080 | tf_op jit(solution)/shard_map/pallas_call | solution.py:227
  162.0 5.4 %fusion.32 = (f32[1024]{0:T(1024)S(1)}, f32[1024,1024]{1,0:T(8,128)S(1)}) fusion(f32[1024]{0:T(1024)S(1)} %bitcast.84, bf16[1024,1024]{1,0:T(8,128)(2,1)} %all-gather.6.cloned.1.call-done, bf16[1024,1024]{1,0:T(8,128)(2,1)} %bitcast.70, bf16[1168,1024]{1,0:T(8,128)(2,1)} %all-gather.4.cloned.1.call-done), kind=kOutput, calls=%fused_computation.100 | convolution fusion | flops 2151676928 | bytes 10493952 | tf_op jit(solution)/shard_map/dot_general | solution.py:40
  172.9 5.1 %convert_reduce_fusion.2 = (f32[1024]{0:T(1024)S(1)}, bf16[1024,1024]{1,0:T(8,128)(2,1)S(1)}) fusion(f32[1024,1024]{1,0:T(8,128)S(1)} %fusion.25, f32[1024]{0:T(1024)S(1)} %convert_element_type.117, bf16[1024,1024]{1,0:T(8,128)(2,1)S(1)} %copy-done.10, bf16[1024,1024]{1,0:T(8,128)(2,1)S(1)} %bitcast.92), kind=kOutput, calls=%fused_computation.26 | convolution fusion | flops 2171599872 | bytes 10493952 | tf_op jit(solution)/shard_map/dot_general | solution.py:315
  179.4 3.7 %convolution_convert_fusion.2 = bf16[1024,1024]{1,0:T(8,128)(2,1)} fusion(bf16[1024,1024]{1,0:T(8,128)(2,1)S(1)} %get-tuple-element.69, bf16[1024,1024]{1,0:T(8,128)(2,1)S(1)} %bitcast.90), kind=kOutput, calls=%fused_computation.43 | convolution fusion | flops 2148532224 | bytes 6291456 | tf_op jit(solution)/shard_map/dot_general | solution.py:40
  183.2 7.0 %convolution_convert_fusion.3 = bf16[1024,1024]{1,0:T(8,128)(2,1)} fusion(bf16[1024,1024]{1,0:T(8,128)(2,1)} %bitcast.91, f32[1024,1024]{1,0:T(8,128)} %copy-done.21, f32[1024]{0:T(1024)S(1)} %convert_element_type.117), kind=kOutput, calls=%fused_computation.44 | convolution fusion | flops 2159017984 | bytes 8392704 | tf_op jit(solution)/shard_map/dot_general | solution.py:40
  190.5 7.1 %convolution_convert_fusion.1 = bf16[1024,1024]{1,0:T(8,128)(2,1)} fusion(bf16[1024,1024]{1,0:T(8,128)(2,1)} %copy-done.23, f32[1024,1024]{1,0:T(8,128)} %copy-done.2, f32[1024]{0:T(1024)S(1)} %bitcast.83, f32[1024]{0:T(1024)S(1)} %bitcast.73, f32[1024]{0:T(1024)S(1)} %add_rsqrt_fusion, f32[1024]{0:T(1024)S(1)} %broadcast_multiply_fusion.2), kind=kOutput, calls=%fused_computation.42 | convolution fusion | flops 2153775104 | bytes 8404992 | tf_op jit(solution)/shard_map/dot_general | solution.py:40
  197.5 3.9 %convolution_convert_fusion = bf16[1024,1024]{1,0:T(8,128)(2,1)} fusion(bf16[1024,1024]{1,0:T(8,128)(2,1)S(1)} %copy-done.11, f32[1024,1024]{1,0:T(8,128)S(1)} %copy-done.22, f32[1024]{0:T(1024)S(1)} %convert_element_type.117), kind=kOutput, calls=%fused_computation.41 | convolution fusion | flops 2159017984 | bytes 8392704 | tf_op jit(solution)/shard_map/dot_general | solution.py:40
  201.4 48.9 %shard_map.257 = (bf16[8,128,1024]{2,1,0:T(8,128)(2,1)}, bf16[8,128,1024]{2,1,0:T(8,128)(2,1)}) custom-call(bf16[8,128,1024]{2,1,0:T(8,128)(2,1)} %bitcast.63, bf16[8,128,1024]{2,1,0:T(8,128)(2,1)} %bitcast.64), custom_call_target="tpu_custom_call" | custom-call | bytes 83886080 | tf_op jit(solution)/shard_map/pallas_call | solution.py:227
  250.3 4.2 %convert_reduce_fusion.4 = (f32[128,1024]{1,0:T(8,128)}, f32[128,1024]{1,0:T(8,128)}) fusion(bf16[8,128,1024]{2,1,0:T(8,128)(2,1)} %get-tuple-element.38, bf16[8,128,1024]{2,1,0:T(8,128)(2,1)} %get-tuple-element.37), kind=kLoop, calls=%fused_computation.30 | loop fusion | flops 3932160 | bytes 5242880 | tf_op jit(solution)/shard_map/reduce_sum | solution.py:255
  254.5 13.9 %all-reduce.3.cloned.1.call-done = bf16[1024,1024]{1,0:T(8,128)(2,1)} async-done(((bf16[1024,1024]{1,0:T(8,128)(2,1)}), bf16[1024,1024]{1,0:T(8,128)(2,1)}) %all-reduce.3.cloned.1.call-update) | async-done | bytes 2097168 | tf_op jit(solution)/shard_map/psum | solution.py:318
  268.4 4.6 %fusion.17 = (f32[1024]{0:T(1024)S(1)}, f32[1024]{0:T(1024)S(1)}, f32[1024]{0:T(1024)S(1)}, f32[1024]{0:T(1024)S(1)}) fusion(bf16[1024,1024]{1,0:T(8,128)(2,1)} %all-reduce.3.cloned.1.call-done, f32[1024,1024]{1,0:T(8,128)} %copy-done.2, f32[1024]{0:T(1024)S(1)} %add_rsqrt_fusion, f32[1024]{0:T(1024)S(1)} %broadcast_multiply_fusion.2, f32[1024]{0:T(1024)S(1)} %bitcast.74), kind=kLoop, calls=%fused_computation.25 | loop fusion | flops 10481664 | bytes 6320128 | tf_op jit(solution)/shard_map/reduce_sum | solution.py:339
  273.1 3.1 convert_reduce_fusion.3
  278.5 12.8 %shard_map.258 = bf16[1024,768]{1,0:T(8,128)(2,1)S(1)} custom-call(s32[1024]{0:T(1024)S(1)} %copy-done, f32[4]{0:T(128)S(1)} %multiply_power_fusion.slope_ref, bf16[1024,768]{1,0:T(8,128)(2,1)S(1)} %add_convert_fusion.2.packed_ref, f32[2,2,1024]{2,1,0:T(2,128)S(1)} %get-tuple-element.40.total_ref, bf16[1024,256]{1,0:T(8,128)(2,1)S(1)} %convolution_convert_fusion.6.grad_ref), custom_call_target="tpu_custom_call" | custom-call | flops 2684354560 | bytes 4718592 | tf_op jit(solution)/shard_map/pallas_call | solution.py:148
  291.3 4.7 %multiply_reduce_fusion.1 = (f32[1024]{0:T(1024)S(1)}, f32[1024]{0:T(1024)S(1)}, f32[1024]{0:T(1024)S(1)}, f32[1024]{0:T(1024)S(1)}, bf16[1024,1024]{1,0:T(8,128)(2,1)}, /*index=5*/f32[1024,1024]{1,0:T(8,128)}) fusion(f32[1024]{0:T(1024)S(1)} %bitcast.80, f32[1024]{0:T(1024)S(1)} %add_rsqrt_fusion.1, f32[1024]{0:T(1024)S(1)} %broadcast_multiply_fusion.3, ...), kind=kOutput, calls=%fused_computation.29 | convolution fusion | flops 1622142976 | bytes 11563008 | tf_op jit(solution)/shard_map/dot_general | solution.py:40
  296.9 6.7 %shard_map.259 = f32[4,32,128]{2,1,0:T(8,128)} custom-call(f32[32,128]{1,0:T(8,128)} %pad_maximum_fusion.refs_0_), custom_call_target="tpu_custom_call" | custom-call | bytes 655360 | tf_op jit(solution)/shard_map/pallas_call | solution.py:227
  305.3 4.1 %convolution_convert_fusion.5 = bf16[1024,256]{1,0:T(8,128)(2,1)} fusion(bf16[1024,256]{1,0:T(8,128)(2,1)} %get-tuple-element.31, f32[1024,1024]{1,0:T(8,128)} %copy-done.1), kind=kOutput, calls=%fused_computation.46 | convolution fusion | flops 538181632 | bytes 5242880 | tf_op jit(solution)/shard_map/dot_general | solution.py:40
  309.5 3.5 convolution_convert_fusion.4
  313.0 27.1 %shard_map.260 = (bf16[8,128,768]{2,1,0:T(8,128)(2,1)}, bf16[8,128,256]{2,1,0:T(8,128)(2,1)}, f32[8,24,128]{2,1,0:T(8,128)}) custom-call(bf16[8,128,768]{2,1,0:T(8,128)(2,1)} %bitcast.66, bf16[8,128,256]{2,1,0:T(8,128)(2,1)} %bitcast.65, f32[24,128]{1,0:T(8,128)} %bitcast.76), custom_call_target="tpu_custom_call" | custom-call | bytes 42926080 | tf_op jit(solution)/shard_map/pallas_call | solution.py:227
  350.4 9.5 %reduce-scatter.5.cloned.1.call-done = bf16[1024,256]{1,0:T(8,128)(2,1)} async-done(((bf16[1024,1024]{1,0:T(8,128)(2,1)}), bf16[1024,256]{1,0:T(8,128)(2,1)}) %reduce-scatter.5.cloned.1.call-update) | async-done | bytes 524304 | tf_op jit(solution)/shard_map/reduce_scatter | solution.py:357
  359.9 3.0 add_convert_fusion.3
  (125 shorter events, 39.7 us)
Async XLA Ops:
  7.2 60.2 %all-gather.4.cloned.1.call-start = ((), (), s32[]{:S(2)}) async-start(), calls=%async_computation.2 | async-start | bytes 2990080 | tf_op jit(solution)/shard_map/all_gather | solution.py:283
  13.4 100.0 %all-gather.8.cloned.1.call-start = ((), (), s32[]{:S(2)}) async-start(), calls=%async_computation.4 | async-start | bytes 2621440 | tf_op jit(solution)/shard_map/all_gather | solution.py:292
  14.2 147.8 %all-gather.6.cloned.1.call-start = ((), (), s32[]{:S(2)}) async-start(), calls=%async_computation.3 | async-start | bytes 2621440 | tf_op jit(solution)/shard_map/all_gather | solution.py:304
  67.4 4.4 %copy-start.5 = (bf16[1168,1024]{1,0:T(8,128)(2,1)S(1)}, bf16[1168,1024]{1,0:T(8,128)(2,1)}, u32[]{:S(2)}) copy-start(bf16[1168,1024]{1,0:T(8,128)(2,1)} %all-gather.4.cloned.1.call-done) | copy-start | bytes 7176196
  67.4 4.4 %copy-start.17 = (bf16[8,128,768]{2,1,0:T(8,128)(2,1)S(1)}, bf16[8,128,768]{2,1,0:T(8,128)(2,1)}, u32[]{:S(2)}) copy-start(bf16[8,128,768]{2,1,0:T(8,128)(2,1)} %get-tuple-element.30) | copy-start | bytes 4718596
  74.0 11.0 %copy-start.12 = (bf16[1024,128]{1,0:T(8,128)(2,1)S(1)}, bf16[1024,128]{1,0:T(8,128)(2,1)}, u32[]{:S(2)}) copy-start(bf16[1024,128]{1,0:T(8,128)(2,1)} %param.27) | copy-start | bytes 786436
  74.0 11.9 %copy-start.14 = (bf16[1024]{0:T(1024)(128)(2,1)S(1)}, bf16[1024]{0:T(1024)(128)(2,1)}, u32[]{:S(2)}) copy-start(bf16[1024]{0:T(1024)(128)(2,1)} %param.26) | copy-start | bytes 6148
  84.8 183.6 %all-reduce.3.cloned.1.call-start = ((), (), s32[]{:S(2)}) async-start(), calls=%async_computation.6 | async-start | bytes 4194304 | tf_op jit(solution)/shard_map/psum | solution.py:318
  167.3 5.6 %copy-start.2 = (f32[1024,1024]{1,0:T(8,128)}, f32[1024,1024]{1,0:T(8,128)S(1)}, u32[]{:S(2)}) copy-start(f32[1024,1024]{1,0:T(8,128)S(1)} %get-tuple-element.94) | copy-start | bytes 12582916
  172.9 5.1 %copy-start.21 = (f32[1024,1024]{1,0:T(8,128)}, f32[1024,1024]{1,0:T(8,128)S(1)}, u32[]{:S(2)}) copy-start(f32[1024,1024]{1,0:T(8,128)S(1)} %fusion.25) | copy-start | bytes 12582916
  183.1 165.0 %reduce-scatter.3.cloned.1.call-start = ((), (), s32[]{:S(2)}) async-start(), calls=%async_computation.5 | async-start | bytes 2621440 | tf_op jit(solution)/shard_map/reduce_scatter | solution.py:321
  190.2 169.7 %reduce-scatter.5.cloned.1.call-start = ((), (), s32[]{:S(2)}) async-start(), calls=%async_computation.7 | async-start | bytes 2621440 | tf_op jit(solution)/shard_map/reduce_scatter | solution.py:357
  190.4 7.1 %copy-start.11 = (bf16[1024,1024]{1,0:T(8,128)(2,1)S(1)}, bf16[1024,1024]{1,0:T(8,128)(2,1)}, u32[]{:S(2)}) copy-start(bf16[1024,1024]{1,0:T(8,128)(2,1)} %all-gather.8.cloned.1.call-done) | copy-start | bytes 6291460
  190.4 7.1 %copy-start.22 = (f32[1024,1024]{1,0:T(8,128)S(1)}, f32[1024,1024]{1,0:T(8,128)}, u32[]{:S(2)}) copy-start(f32[1024,1024]{1,0:T(8,128)} %copy-done.21) | copy-start | bytes 12582916
  268.4 4.6 %copy-start.3 = (f32[1024,1024]{1,0:T(8,128)S(1)}, f32[1024,1024]{1,0:T(8,128)}, u32[]{:S(2)}) copy-start(f32[1024,1024]{1,0:T(8,128)} %copy-done.2) | copy-start | bytes 12582916
  268.4 4.7 %copy-start.4 = (bf16[1024,1024]{1,0:T(8,128)(2,1)S(1)}, bf16[1024,1024]{1,0:T(8,128)(2,1)}, u32[]{:S(2)}) copy-start(bf16[1024,1024]{1,0:T(8,128)(2,1)} %all-reduce.3.cloned.1.call-done) | copy-start | bytes 6291460
  278.4 12.8 %copy-start.6 = (bf16[1168,1024]{1,0:T(8,128)(2,1)S(1)}, bf16[1168,1024]{1,0:T(8,128)(2,1)}, u32[]{:S(2)}) copy-start(bf16[1168,1024]{1,0:T(8,128)(2,1)} %all-gather.4.cloned.1.call-done) | copy-start | bytes 7176196
  278.4 12.8 %copy-start.18 = (bf16[8,128,768]{2,1,0:T(8,128)(2,1)S(1)}, bf16[8,128,768]{2,1,0:T(8,128)(2,1)}, u32[]{:S(2)}) copy-start(bf16[8,128,768]{2,1,0:T(8,128)(2,1)} %get-tuple-element.30) | copy-start | bytes 4718596
  291.3 4.7 %copy-start.9 = (bf16[1024,256]{1,0:T(8,128)(2,1)S(1)}, bf16[1024,256]{1,0:T(8,128)(2,1)}, u32[]{:S(2)}) copy-start(bf16[1024,256]{1,0:T(8,128)(2,1)} %param.29) | copy-start | bytes 1572868
  291.3 4.9 %copy-start.19 = (bf16[256]{0:T(256)(128)(2,1)S(1)}, bf16[256]{0:T(256)(128)(2,1)}, u32[]{:S(2)}) copy-start(bf16[256]{0:T(256)(128)(2,1)} %param.17) | copy-start | bytes 1540
  291.3 4.9 %copy-start.20 = (bf16[256]{0:T(256)(128)(2,1)S(1)}, bf16[256]{0:T(256)(128)(2,1)}, u32[]{:S(2)}) copy-start(bf16[256]{0:T(256)(128)(2,1)} %param.28) | copy-start | bytes 1540
  304.9 4.6 %copy-start.7 = (bf16[1168,1024]{1,0:T(8,128)(2,1)S(1)}, bf16[1168,1024]{1,0:T(8,128)(2,1)}, u32[]{:S(2)}) copy-start(bf16[1168,1024]{1,0:T(8,128)(2,1)} %all-gather.4.cloned.1.call-done) | copy-start | bytes 7176196
  305.3 7.7 %copy-start.13 = (f32[3072]{0:T(1024)}, f32[3072]{0:T(1024)S(1)}, u32[]{:S(2)}) copy-start(f32[3072]{0:T(1024)S(1)} %constant_dynamic-update-slice_fusion) | copy-start | bytes 36868
  309.5 33.5 %copy-start.8 = (f32[128,1024]{1,0:T(8,128)S(1)}, f32[128,1024]{1,0:T(8,128)}, u32[]{:S(2)}) copy-start(f32[128,1024]{1,0:T(8,128)} %get-tuple-element.45) | copy-start | bytes 1572868
  (6 other events, 13.8 us)
Sparse Core Ops, SparseCore 0:
  13.6 53.7 all-gather.3
  68.9 44.4 all-gather.7
  115.5 44.4 all-gather.5
  183.2 85.1 all-reduce.2
  270.6 43.8 reduce-scatter.2
  316.7 43.1 reduce-scatter.4

commit v4 on v3

--- a/solution.py
+++ b/solution.py
@@ -242,8 +242,93 @@
     )(*sources)
 
 
+def gather_body(count, devices, *refs):
+    sources, results = refs[:count], refs[count : 2 * count]
+    local_sem, send_sem, recv_sem = refs[2 * count :]
+    me = lax.axis_index("wide")
+    beside = me + 1 - 2 * lax.rem(me, 2)
+    steps = devices // 2
+
+    barrier = pltpu.get_barrier_semaphore()
+
+    def signal(peer):
+        pl.semaphore_signal(
+            barrier, inc=1, device_id={"wide": peer}, device_id_type=pl.DeviceIdType.MESH
+        )
+
+    def greet(step, carry):
+        signal(lax.rem(me + 2 * step, devices))
+        return carry
+
+    lax.fori_loop(1, steps, greet, 0)
+    signal(beside)
+    pl.semaphore_wait(barrier, steps)
+
+    def copy(item, source, slot, peer, index):
+        return pltpu.make_async_remote_copy(
+            src_ref=source,
+            dst_ref=results[item].at[slot],
+            send_sem=send_sem.at[item, index],
+            recv_sem=recv_sem.at[item, index],
+            device_id={"wide": peer},
+            device_id_type=pl.DeviceIdType.MESH,
+        )
+
+    def copy_to(item, step):
+        peer = lax.rem(me + 2 * step, devices)
+        return copy(item, sources[item], me, peer, step)
+
+    def pass_on(item, step):
+        slot = lax.rem(me + devices - 2 * step, devices)
+        return copy(item, results[item].at[slot], slot, beside, steps + step)
+
+    def start(step, carry):
+        for item in range(count):
+            copy_to(item, step).start()
+        return carry
+
+    def forward(step, carry):
+        for item in range(count):
+            copy_to(item, step).wait_recv()
+            pass_on(item, step).start()
+        return carry
+
+    def finish(step, carry):
+        for item in range(count):
+            copy_to(item, step).wait_send()
+            pass_on(item, step).wait()
+        return carry
+
+    lax.fori_loop(1, steps, start, 0)
+    for item in range(count):
+        copy(item, sources[item], me, beside, 0).start()
+    for item in range(count):
+        own = pltpu.make_async_copy(sources[item], results[item].at[me], local_sem.at[item])
+        own.start()
+        own.wait()
+    lax.fori_loop(1, steps, forward, 0)
+    for item in range(count):
+        copy(item, sources[item], me, beside, 0).wait()
+    lax.fori_loop(1, steps, finish, 0)
+
+
 def gather_rows(sources, call_id):
-    gathered = exchange(sources, (False,) * len(sources), "wide", call_id)
+    devices = lax.axis_size("wide")
+    count = len(sources)
+    size = sum(2 * devices * item.size for item in sources)
+    gathered = pl.pallas_call(
+        partial(gather_body, count, devices),
+        in_specs=[pl.BlockSpec(memory_space=pl.ANY)] * count,
+        out_specs=[pl.BlockSpec(memory_space=pl.ANY)] * count,
+        out_shape=[jax.ShapeDtypeStruct((devices, *item.shape), item.dtype) for item in sources],
+        scratch_shapes=[
+            pltpu.SemaphoreType.DMA((count,)),
+            pltpu.SemaphoreType.DMA((count, devices)),
+            pltpu.SemaphoreType.DMA((count, devices)),
+        ],
+        compiler_params=pltpu.CompilerParams(collective_id=call_id, has_side_effects=True),
+        cost_estimate=pl.CostEstimate(flops=0, bytes_accessed=10 * size, transcendentals=0),
+    )(*sources)
     return [item.reshape(-1, item.shape[-1]) for item in gathered]
 
 
@@ -301,55 +386,86 @@
         jnp.dot(act_one, qkv_full, preferred_element_type=jnp.float32) + full_bias[None]
     ).astype(jnp.bfloat16)
     attended, log_totals = attend_forward(packed, slopes, segments)
-    attended_full = lax.all_gather(attended, "narrow", axis=1, tiled=True)
+    half_rows = tok_rows // 2
+    spans = [slice(0, half_rows), slice(half_rows, tok_rows)]
+    attended_halves = [
+        lax.all_gather(attended[span], "narrow", axis=1, tiled=True) for span in spans
+    ]
     dense_block, grad_out = lax.optimization_barrier((dense_block, grad_out))
     dense_rows, down_rows = gather_rows([dense_block, down_weight.T], 1)
-    mixed = contract(attended_full, dense_rows, 1, 1)
-    residual = inputs + (mixed + bias_dense)
-    normed_two, hat_two, inv_two = normalize(residual, gain_two, shift_two)
-    act_two = normed_two.astype(jnp.bfloat16)
-    pre_act = jnp.dot(act_two, up_full, preferred_element_type=jnp.float32) + up_bias.astype(
-        jnp.float32
-    )
-    hidden = jax.nn.gelu(pre_act, approximate=True).astype(jnp.bfloat16)
-    grad_hidden = jnp.dot(grad_out, down_rows, preferred_element_type=jnp.float32)
-    _, gelu_back = jax.vjp(partial(jax.nn.gelu, approximate=True), pre_act)
-    grad_pre = gelu_back(grad_hidden)[0].astype(jnp.bfloat16)
-    grad_act_two = lax.psum(
-        contract(grad_pre, up_full, 1, 1).astype(jnp.bfloat16), "narrow"
-    )
+    kept = []
+    grad_parts = []
+    for span, attended_half in zip(spans, attended_halves):
+        if grad_parts:
+            attended_half, _ = lax.optimization_barrier((attended_half, grad_parts[0]))
+        mixed = contract(attended_half, dense_rows, 1, 1)
+        residual = inputs[span] + (mixed + bias_dense)
+        normed_two, hat_two, inv_two = normalize(residual, gain_two, shift_two)
+        act_two = normed_two.astype(jnp.bfloat16)
+        pre_act = jnp.dot(act_two, up_full, preferred_element_type=jnp.float32) + up_bias.astype(
+            jnp.float32
+        )
+        hidden = jax.nn.gelu(pre_act, approximate=True).astype(jnp.bfloat16)
+        grad_hidden = jnp.dot(grad_out[span], down_rows, preferred_element_type=jnp.float32)
+        _, gelu_back = jax.vjp(partial(jax.nn.gelu, approximate=True), pre_act)
+        grad_pre = gelu_back(grad_hidden)[0].astype(jnp.bfloat16)
+        grad_parts.append(contract(grad_pre, up_full, 1, 1).astype(jnp.bfloat16))
+        kept.append(
+            (own_columns(residual, col_start, local_width), hat_two, inv_two, act_two, hidden, grad_pre)
+        )
+    grad_twos = [lax.psum(grad_parts[0], "narrow")]
+    grad_parts[1], grad_twos[0] = lax.optimization_barrier((grad_parts[1], grad_twos[0]))
+    grad_twos.append(lax.psum(grad_parts[1], "narrow"))
+    own_residual, act_two, hidden, grad_pre = (
+        jnp.concatenate([kept[0][item], kept[1][item]], axis=0) for item in (0, 3, 4, 5)
+    )
+    mlp_part = contract(hidden, down_rows, 1, 1).astype(jnp.bfloat16)
+    mlp_part, grad_twos[1] = lax.optimization_barrier((mlp_part, grad_twos[1]))
     mlp_out = lax.psum_scatter(
-        contract(hidden, down_rows, 1, 1).astype(jnp.bfloat16),
+        mlp_part,
         "narrow",
         scatter_dimension=1,
         tiled=True,
     ).astype(jnp.float32)
     output = (
-        own_columns(residual, col_start, local_width) + (mlp_out + down_bias.astype(jnp.float32))
+        own_residual + (mlp_out + down_bias.astype(jnp.float32))
     ).astype(jnp.bfloat16)
     down_bias_grad = jnp.sum(cotangent.astype(jnp.float32), axis=0)
     up_bias_grad = jnp.sum(grad_pre.astype(jnp.float32), axis=0)
     grad_down = contract(grad_out, hidden, 0, 0).astype(jnp.bfloat16)
     grad_up = contract(act_two, grad_pre, 0, 0).astype(jnp.bfloat16)
     up_weight_grad, down_rows_grad = scatter_sums([grad_up, grad_down], 2)
-    grad_act_two, up_weight_grad, down_rows_grad = lax.optimization_barrier(
-        (grad_act_two, up_weight_grad, down_rows_grad)
-    )
-    grad_act_two = grad_act_two.astype(jnp.float32)
-    second_gain_grad = own_columns(jnp.sum(grad_act_two * hat_two, axis=0), col_start, local_width)
-    second_shift_grad = own_columns(jnp.sum(grad_act_two, axis=0), col_start, local_width)
-    grad_residual = grad_out.astype(jnp.float32) + norm_backward(
-        grad_act_two, gain_two, hat_two, inv_two
-    )
-    grad_branch = grad_residual.astype(jnp.bfloat16)
-    dense_bias_grad = own_columns(
-        jnp.sum(grad_branch.astype(jnp.float32), axis=0), col_start, local_width
-    )
-    grad_attended = jnp.dot(
-        grad_branch,
-        own_columns(dense_rows, col_start, local_width),
-        preferred_element_type=jnp.float32,
-    ).astype(jnp.bfloat16)
+    grad_twos[1], up_weight_grad, down_rows_grad = lax.optimization_barrier(
+        (grad_twos[1], up_weight_grad, down_rows_grad)
+    )
+    dense_own = own_columns(dense_rows, col_start, local_width)
+    back = []
+    sums = []
+    for span, grad_two, (_, hat_two, inv_two, _, _, _) in zip(spans, grad_twos, kept):
+        grad_act_two = grad_two.astype(jnp.float32)
+        grad_residual = grad_out[span].astype(jnp.float32) + norm_backward(
+            grad_act_two, gain_two, hat_two, inv_two
+        )
+        grad_branch = grad_residual.astype(jnp.bfloat16)
+        sums.append(
+            (
+                jnp.sum(grad_act_two * hat_two, axis=0),
+                jnp.sum(grad_act_two, axis=0),
+                jnp.sum(grad_branch.astype(jnp.float32), axis=0),
+            )
+        )
+        grad_attended = jnp.dot(
+            grad_branch, dense_own, preferred_element_type=jnp.float32
+        ).astype(jnp.bfloat16)
+        back.append(
+            (own_columns(grad_residual, col_start, local_width), grad_branch, grad_attended)
+        )
+    own_grad_residual, grad_branch, grad_attended = (
+        jnp.concatenate(pair, axis=0) for pair in zip(*back)
+    )
+    second_gain_grad, second_shift_grad, dense_bias_grad = (
+        own_columns(low + high, col_start, local_width) for low, high in zip(*sums)
+    )
     grad_packed = attend_backward(packed, slopes, segments, log_totals, grad_attended)
     column_sums = jnp.sum(grad_packed.astype(jnp.float32), axis=0).reshape(heads_here, 3, HD)
     qv_bias_grad = jnp.stack([column_sums[:, 0], column_sums[:, 2]], axis=1).reshape(-1)
@@ -402,7 +518,7 @@
     grad_norm_one = inv_one * (
         scaled - sum_plain[:, None] / full_width - hat_local * sum_hat[:, None] / full_width
     )
-    token_grad = (own_columns(grad_residual, col_start, local_width) + grad_norm_one).astype(
+    token_grad = (own_grad_residual + grad_norm_one).astype(
         jnp.bfloat16
     )
     dense_weight_grad = dense_rows_grad.T

time: 376 us -> 438 us (1.16)
  waiting for transfers between devices: 57.8 us -> 145 us
  Pallas kernels: 199 us -> 160 us
  local copies, waits for them, and re-layouts: 15.8 us -> 22.3 us
    pallas_call x5 -> x3, Pallas kernels: 176 us -> 81.2 us  [exchange(): pl.pallas_call(partial(exchange_body, scatter, axis, devices), in_specs=[...]
    psum x1 -> x2, waiting for transfers between devices: 13.9 us -> 77.6 us  [the longest x1 41.2 us: local(): grad_twos.append(lax.psum(grad_parts[1], 'narrow'))]
    pallas_call x0 -> x2, Pallas kernels: none -> 56.3 us  [gather_rows(): pl.pallas_call(partial(gather_body, count, devices), in_specs=[pl.BlockSp...]
    all_gather x1, waiting for transfers between devices: 7.73 us -> 25.5 us  [local(): lax.all_gather(jnp.concatenate([tokens, dense_weight.T, vectors], axis=0)...]
    all_gather x1 -> x2, waiting for transfers between devices: 0.02 us -> 14.8 us  [local(): lax.all_gather(attended[span], 'narrow', axis=1, tiled=True)]
    reduce_scatter x1, waiting for transfers between devices: 9.51 us -> 0.01 us  [local(): lax.psum_scatter(grad_one_part.astype(jnp.bfloat16), 'narrow', scatter_di...]
    unnamed x59 -> x87, local copies, waits for them, and re-layouts: 7.97 us -> 12 us
    dot_general x8 -> x10, matrix products: 39.3 us -> 41.9 us  [contract(): lax.dot_general(left, right, (((left_dim,), (right_dim,)), ((), ())), pre...]
  transfers between devices with their start and end apart: 6 -> 8, of which waited for: 4 -> 5; matrix products, arithmetic and copies ran while one was open for 18% -> 21% of each run, Pallas kernels for 54% -> 37%
where the time goes in v4:
time: 438 us; the launch traced here: 431 us
  Pallas kernels  160 us (37%)
  waiting for transfers between devices  145 us (33%)
  matrix products  54.3 us (12%)
  other arithmetic  32.6 us (7%)
  local copies, waits for them, and re-layouts  22.3 us (5%)
  between operations  15 us (3%)
    pallas_call x3, Pallas kernels, exchange(): pl.pallas_call(partial(exchange_body, scatter, axis, devices), in_specs=[...  81.2 us
    pallas_call x2, Pallas kernels, gather_rows(): pl.pallas_call(partial(gather_body, count, devices), in_specs=[pl.BlockSp...  56.3 us
    dot_general x10, matrix products, contract(): lax.dot_general(left, right, (((left_dim,), (right_dim,)), ((), ())), pre...  41.9 us
    psum x1, waiting for transfers between devices, local(): grad_twos.append(lax.psum(grad_parts[1], 'narrow'))  41.2 us
    psum x1, waiting for transfers between devices, local(): grad_twos = [lax.psum(grad_parts[0], 'narrow')]  36.4 us
    all_gather x1, waiting for transfers between devices, local(): grad_out = lax.all_gather(cotangent, 'narrow', axis=1, tiled=True)  26.8 us
    all_gather x1, waiting for transfers between devices, local(): lax.all_gather(jnp.concatenate([tokens, dense_weight.T, vectors], axis=0)...  25.5 us
    all_gather x2, waiting for transfers between devices, local(): lax.all_gather(attended[span], 'narrow', axis=1, tiled=True)  14.8 us
  transfers between devices with their start and end apart: 8, of which 5 were waited for; matrix products, arithmetic and copies ran while one was open for 21% of the time, Pallas kernels for 37%

profile of v4, /device:TPU:0, one launch (start us, length us, event | category | flops | bytes accessed | tf_op | source)
XLA Modules:
  0.0 431.1 jit_solution(10470014023899675581)
XLA Ops:
  14.5 27.3 %shard_map.254 = (bf16[8,128,768]{2,1,0:T(8,128)(2,1)}, bf16[8,128,1024]{2,1,0:T(8,128)(2,1)}) custom-call(bf16[128,768]{1,0:T(8,128)(2,1)} %refs_0_.1, bf16[128,1024]{1,0:T(8,128)(2,1)} %refs_1_.1), custom_call_target="tpu_custom_call" | custom-call | bytes 36700160 | tf_op jit(solution)/shard_map/pallas_call | solution.py:319
  41.9 25.5 %all-gather.5.cloned.1.call-done = bf16[1168,1024]{1,0:T(8,128)(2,1)} async-done(((bf16[1168,256]{1,0:T(8,128)(2,1)}), bf16[1168,1024]{1,0:T(8,128)(2,1)}) %all-gather.5.cloned.1.call-update) | async-done | bytes 2392080 | tf_op jit(solution)/shard_map/all_gather | solution.py:368
  74.0 10.1 %shard_map.255 = (bf16[1024,256]{1,0:T(8,128)(2,1)S(1)}, f32[2,2,1024]{2,1,0:T(2,128)S(1)}) custom-call(s32[1024]{0:T(1024)S(1)} %copy-done, f32[4]{0:T(128)S(1)} %multiply_power_fusion.slope_ref, bf16[1024,768]{1,0:T(8,128)(2,1)S(1)} %add_convert_fusion.1.packed_ref), custom_call_target="tpu_custom_call" | custom-call | flops 1073741824 | bytes 3145728 | tf_op jit(solution)/shard_map/pallas_call | solution.py:126
  86.6 26.8 %all-gather.9.cloned.1.call-done = bf16[1024,1024]{1,0:T(8,128)(2,1)} async-done(((bf16[1024,256]{1,0:T(8,128)(2,1)}), bf16[1024,1024]{1,0:T(8,128)(2,1)}) %all-gather.9.cloned.1.call-update) | async-done | bytes 2097168 | tf_op jit(solution)/shard_map/all_gather | solution.py:377
  113.4 29.0 %shard_map.256 = (bf16[8,128,1024]{2,1,0:T(8,128)(2,1)}, bf16[8,128,1024]{2,1,0:T(8,128)(2,1)}) custom-call(bf16[128,1024]{1,0:T(8,128)(2,1)} %slice.152.refs_0_, bf16[128,1024]{1,0:T(8,128)(2,1)} %bitcast.74), custom_call_target="tpu_custom_call" | custom-call | bytes 41943040 | tf_op jit(solution)/shard_map/pallas_call | solution.py:319
  145.1 3.9 fusion.70
  159.7 14.8 %all-gather.11.cloned.1.call-done = bf16[512,1024]{1,0:T(8,128)(2,1)} async-done(((bf16[512,256]{1,0:T(8,128)(2,1)}), bf16[512,1024]{1,0:T(8,128)(2,1)}) %all-gather.11.cloned.1.call-update) | async-done | bytes 1048592 | tf_op jit(solution)/shard_map/all_gather | solution.py:392
  175.0 3.9 fusion.71
  181.4 3.4 multiply_convert_fusion.1
  190.5 36.4 %all-reduce.4.cloned.1.call-done = bf16[512,1024]{1,0:T(8,128)(2,1)} async-done(((bf16[512,1024]{1,0:T(8,128)(2,1)}), bf16[512,1024]{1,0:T(8,128)(2,1)}) %all-reduce.4.cloned.1.call-update) | async-done | bytes 1048592 | tf_op jit(solution)/shard_map/psum | solution.py:416
  227.2 6.0 %convolution_convert_fusion.1 = bf16[1024,1024]{1,0:T(8,128)(2,1)} fusion(bf16[1024,1024]{1,0:T(8,128)(2,1)} %bitcast.104, bf16[512,1024]{1,0:T(8,128)(2,1)} %get-tuple-element.117, bf16[512,1024]{1,0:T(8,128)(2,1)} %get-tuple-element.116), kind=kOutput, calls=%fused_computation.77 | convolution fusion | flops 2152726528 | bytes 6291456 | tf_op jit(solution)/shard_map/dot_general | solution.py:40
  233.2 6.1 %convolution_convert_fusion = bf16[1024,1024]{1,0:T(8,128)(2,1)} fusion(bf16[1024,1024]{1,0:T(8,128)(2,1)} %all-gather.9.cloned.1.call-done, bf16[512,1024]{1,0:T(8,128)(2,1)} %get-tuple-element.117, bf16[512,1024]{1,0:T(8,128)(2,1)} %get-tuple-element.116), kind=kOutput, calls=%fused_computation.76 | convolution fusion | flops 2152726528 | bytes 6291456 | tf_op jit(solution)/shard_map/dot_general | solution.py:40
  239.3 41.2 %all-reduce.6.cloned.1.call-done = bf16[512,1024]{1,0:T(8,128)(2,1)} async-done(((bf16[512,1024]{1,0:T(8,128)(2,1)}), bf16[512,1024]{1,0:T(8,128)(2,1)}) %all-reduce.6.cloned.1.call-update) | async-done | bytes 1048592 | tf_op jit(solution)/shard_map/psum | solution.py:418
  280.5 5.9 %fusion.38 = bf16[1024,1024]{1,0:T(8,128)(2,1)} fusion(bf16[512,1024]{1,0:T(8,128)(2,1)} %copy-done.22, bf16[512,1024]{1,0:T(8,128)(2,1)} %copy-done.20, bf16[512,1024]{1,0:T(8,128)(2,1)} %copy-done.21, bf16[512,1024]{1,0:T(8,128)(2,1)} %copy-done.19), kind=kOutput, calls=%fused_computation.75 | convolution fusion | flops 2156920832 | bytes 6291456 | tf_op jit(solution)/shard_map/dot_general | solution.py:40
  286.4 48.7 %shard_map.257 = (bf16[8,128,1024]{2,1,0:T(8,128)(2,1)}, bf16[8,128,1024]{2,1,0:T(8,128)(2,1)}) custom-call(bf16[8,128,1024]{2,1,0:T(8,128)(2,1)} %bitcast.72, bf16[8,128,1024]{2,1,0:T(8,128)(2,1)} %bitcast.71), custom_call_target="tpu_custom_call" | custom-call | bytes 83886080 | tf_op jit(solution)/shard_map/pallas_call | solution.py:227
  338.4 3.6 convert_reduce_fusion.1
  344.3 3.4 convert_reduce_fusion.9
  349.8 12.8 %shard_map.258 = bf16[1024,768]{1,0:T(8,128)(2,1)S(1)} custom-call(s32[1024]{0:T(1024)S(1)} %copy-done, f32[4]{0:T(128)S(1)} %multiply_power_fusion.slope_ref, bf16[1024,768]{1,0:T(8,128)(2,1)S(1)} %copy-done.2, f32[2,2,1024]{2,1,0:T(2,128)S(1)} %get-tuple-element.50.total_ref, bf16[1024,256]{1,0:T(8,128)(2,1)S(1)} %pad_maximum_fusion.5.grad_ref), custom_call_target="tpu_custom_call" | custom-call | flops 2684354560 | bytes 4718592 | tf_op jit(solution)/shard_map/pallas_call | solution.py:148
  362.7 4.7 %multiply_reduce_fusion.1 = (f32[1024]{0:T(1024)S(1)}, f32[1024]{0:T(1024)S(1)}, f32[1024]{0:T(1024)S(1)}, f32[1024]{0:T(1024)S(1)}, bf16[1024,1024]{1,0:T(8,128)(2,1)}, /*index=5*/f32[1024,1024]{1,0:T(8,128)}) fusion(f32[1024]{0:T(1024)S(1)} %bitcast.88, f32[1024]{0:T(1024)S(1)} %add_rsqrt_fusion, f32[1024]{0:T(1024)S(1)} %broadcast_multiply_fusion, ...), kind=kOutput, calls=%fused_computation.2 | convolution fusion | flops 1622142976 | bytes 11563008 | tf_op jit(solution)/shard_map/dot_general | solution.py:40
  369.5 6.3 %shard_map.259 = f32[4,32,128]{2,1,0:T(8,128)} custom-call(f32[32,128]{1,0:T(8,128)} %pad_maximum_fusion.6.refs_0_), custom_call_target="tpu_custom_call" | custom-call | bytes 655360 | tf_op jit(solution)/shard_map/pallas_call | solution.py:227
  377.1 3.3 fusion.41
  380.4 3.5 convolution_convert_fusion.2
  383.9 26.2 %shard_map.260 = (bf16[8,128,768]{2,1,0:T(8,128)(2,1)}, bf16[8,128,256]{2,1,0:T(8,128)(2,1)}, f32[8,24,128]{2,1,0:T(8,128)}) custom-call(bf16[8,128,768]{2,1,0:T(8,128)(2,1)} %bitcast.73, bf16[8,128,256]{2,1,0:T(8,128)(2,1)} %bitcast.76, f32[24,128]{1,0:T(8,128)} %bitcast.84), custom_call_target="tpu_custom_call" | custom-call | bytes 42926080 | tf_op jit(solution)/shard_map/pallas_call | solution.py:227
  421.3 2.7 fusion.46
  (181 shorter events, 60.7 us)
Async XLA Ops:
  7.2 7.0 %copy-start.26 = (bf16[512]{0:T(512)(128)(2,1)S(1)}, bf16[512]{0:T(512)(128)(2,1)}, u32[]{:S(2)}) copy-start(bf16[512]{0:T(512)(128)(2,1)} %param.20) | copy-start | bytes 3076
  7.2 60.2 %all-gather.5.cloned.1.call-start = ((), (), s32[]{:S(2)}) async-start(), calls=%async_computation.2 | async-start | bytes 2990080 | tf_op jit(solution)/shard_map/all_gather | solution.py:368
  13.4 100.0 %all-gather.9.cloned.1.call-start = ((), (), s32[]{:S(2)}) async-start(), calls=%async_computation.4 | async-start | bytes 2621440 | tf_op jit(solution)/shard_map/all_gather | solution.py:377
  14.2 130.9 %all-gather.7.cloned.1.call-start = ((), (), s32[]{:S(2)}) async-start(), calls=%async_computation.3 | async-start | bytes 1310720 | tf_op jit(solution)/shard_map/all_gather | solution.py:392
  67.4 4.4 %copy-start.5 = (bf16[1168,1024]{1,0:T(8,128)(2,1)S(1)}, bf16[1168,1024]{1,0:T(8,128)(2,1)}, u32[]{:S(2)}) copy-start(bf16[1168,1024]{1,0:T(8,128)(2,1)} %all-gather.5.cloned.1.call-done) | copy-start | bytes 7176196
  67.4 4.4 %copy-start.32 = (bf16[8,128,768]{2,1,0:T(8,128)(2,1)S(1)}, bf16[8,128,768]{2,1,0:T(8,128)(2,1)}, u32[]{:S(2)}) copy-start(bf16[8,128,768]{2,1,0:T(8,128)(2,1)} %get-tuple-element.35) | copy-start | bytes 4718596
  74.0 10.2 %copy-start.1 = (bf16[1024,768]{1,0:T(8,128)(2,1)}, bf16[1024,768]{1,0:T(8,128)(2,1)S(1)}, u32[]{:S(2)}) copy-start(bf16[1024,768]{1,0:T(8,128)(2,1)S(1)} %add_convert_fusion.1.packed_ref) | copy-start | bytes 4718596
  74.0 11.1 %copy-start.25 = (bf16[1024]{0:T(1024)(128)(2,1)S(1)}, bf16[1024]{0:T(1024)(128)(2,1)}, u32[]{:S(2)}) copy-start(bf16[1024]{0:T(1024)(128)(2,1)} %param.26) | copy-start | bytes 6148
  74.0 11.1 %copy-start.23 = (bf16[1024,128]{1,0:T(8,128)(2,1)S(1)}, bf16[1024,128]{1,0:T(8,128)(2,1)}, u32[]{:S(2)}) copy-start(bf16[1024,128]{1,0:T(8,128)(2,1)} %param.27) | copy-start | bytes 786436
  85.0 89.6 %all-gather.11.cloned.1.call-start = ((), (), s32[]{:S(2)}) async-start(), calls=%async_computation.5 | async-start | bytes 1310720 | tf_op jit(solution)/shard_map/all_gather | solution.py:392
  142.4 84.5 %all-reduce.4.cloned.1.call-start = ((), (), s32[]{:S(2)}) async-start(), calls=%async_computation.6 | async-start | bytes 2097152 | tf_op jit(solution)/shard_map/psum | solution.py:416
  152.8 3.5 copy-start.36
  174.6 105.9 %all-reduce.6.cloned.1.call-start = ((), (), s32[]{:S(2)}) async-start(), calls=%async_computation.7 | async-start | bytes 2097152 | tf_op jit(solution)/shard_map/psum | solution.py:418
  188.2 38.8 %copy-start.11 = (bf16[1024,256]{1,0:T(8,128)(2,1)S(1)}, bf16[1024,256]{1,0:T(8,128)(2,1)}, u32[]{:S(2)}) copy-start(bf16[1024,256]{1,0:T(8,128)(2,1)} %param.29) | copy-start | bytes 1572868
  188.2 38.9 %copy-start.34 = (bf16[256]{0:T(256)(128)(2,1)S(1)}, bf16[256]{0:T(256)(128)(2,1)}, u32[]{:S(2)}) copy-start(bf16[256]{0:T(256)(128)(2,1)} %param.17) | copy-start | bytes 1540
  188.2 39.0 %copy-start.35 = (bf16[256]{0:T(256)(128)(2,1)S(1)}, bf16[256]{0:T(256)(128)(2,1)}, u32[]{:S(2)}) copy-start(bf16[256]{0:T(256)(128)(2,1)} %param.28) | copy-start | bytes 1540
  226.9 192.4 %reduce-scatter.3.cloned.1.call-start = ((), (), s32[]{:S(2)}) async-start(), calls=%async_computation.8 | async-start | bytes 2621440 | tf_op jit(solution)/shard_map/reduce_scatter | solution.py:424
  280.5 140.8 %reduce-scatter.5.cloned.1.call-start = ((), (), s32[]{:S(2)}) async-start(), calls=%async_computation.9 | async-start | bytes 2621440 | tf_op jit(solution)/shard_map/reduce_scatter | solution.py:473
  338.4 3.6 copy-start.8
  338.4 3.6 copy-start.9
  349.8 12.8 %copy-start.6 = (bf16[1168,1024]{1,0:T(8,128)(2,1)S(1)}, bf16[1168,1024]{1,0:T(8,128)(2,1)}, u32[]{:S(2)}) copy-start(bf16[1168,1024]{1,0:T(8,128)(2,1)} %all-gather.5.cloned.1.call-done) | copy-start | bytes 7176196
  349.8 12.8 %copy-start.33 = (bf16[8,128,768]{2,1,0:T(8,128)(2,1)S(1)}, bf16[8,128,768]{2,1,0:T(8,128)(2,1)}, u32[]{:S(2)}) copy-start(bf16[8,128,768]{2,1,0:T(8,128)(2,1)} %get-tuple-element.35) | copy-start | bytes 4718596
  412.9 6.4 %copy-start.12 = (f32[512,256]{1,0:T(8,128)S(1)}, f32[512,256]{1,0:T(8,128)}, u32[]{:S(2)}) copy-start(f32[512,256]{1,0:T(8,128)} %get-tuple-element.128) | copy-start | bytes 1572868
  412.9 6.4 %copy-start.13 = (f32[512,256]{1,0:T(8,128)S(1)}, f32[512,256]{1,0:T(8,128)}, u32[]{:S(2)}) copy-start(f32[512,256]{1,0:T(8,128)} %get-tuple-element.129) | copy-start | bytes 1572868
  (22 other events, 50.4 us)
Sparse Core Ops, SparseCore 0:
  13.5 53.7 all-gather.4
  68.9 44.4 all-gather.8
  115.5 28.4 all-gather.6
  146.0 28.5 all-gather.10
  176.7 50.1 all-reduce.3
  229.2 51.1 all-reduce.5
  282.8 43.2 reduce-scatter.2
  367.5 43.6 reduce-scatter.4
